TPU v7x, 32 devices: a whole 2x2x4 slice. The times are simulated.
32 devices in a mesh: dp: 4 (over x, core), wide: 8 (over z, y).
Axes of the slice: x: 2, y: 2, z: 4, core: 2. Of those that a mesh axis runs over, the one named last changes fastest.
Arguments:
- tokens: bfloat16 [32768, 16384], P('dp', 'wide'), may hold values from -6 to 6
- cotangent: bfloat16 [32768, 16384], P('dp', 'wide'), may hold values from -6 to 6
- left_factor: bfloat16 [128, 128, 128], P('wide', 'dp'), may hold values from -0.5 to 0.5
- right_factor: bfloat16 [128, 128, 128], P('wide', 'dp'), may hold values from -0.5 to 0.5
- column_map: int32 [16384], replicated, may hold values from 0 to 16383, as said below
Outputs:
- grad_tokens: bfloat16 [32768, 16384], P('dp', 'wide')
- grad_left: float32 [128, 128, 128], P('wide', 'dp')
- grad_right: float32 [128, 128, 128], P('wide', 'dp')
Inputs may be any that keep to these rules, and one draw needn't show every extreme that they name: column_map[c * 128 + r] = block_order[r] * 128 + lane_order[c] for two permutations block_order and lane_order of 0 to 127: column r of output block c takes lane lane_order[c] of input block block_order[r].
All inputs are finite; a program needn't handle non-finite values.
Results may differ from a plain program's by a relative error of at most 0.0057.
Values may be sent and summed in bfloat16 or wider, within the bound.
No kernel may reach another device: no remote copies, remote signals or barrier semaphores. Data moves between devices by JAX's collectives and lax.ppermute only.
A program may use at most 256 MiB of HBM per device.

v0:
```python
import jax
import jax.numpy as jnp
from jax import lax
from jax.sharding import PartitionSpec as P

gelu_scale = 0.7978845608
gelu_cubic = 0.044715


def gelu_parts(value):
    tanh_part = jnp.tanh(gelu_scale * (value + gelu_cubic * value * value * value))
    result = 0.5 * value * (1.0 + tanh_part)
    slope = 0.5 * (1.0 + tanh_part) + 0.5 * value * (1.0 - tanh_part * tanh_part) * gelu_scale * (
        1.0 + 3.0 * gelu_cubic * value * value
    )
    return (result, slope)


def shards(tokens, cotangent, left_factor, right_factor, column_map):
    row_count = tokens.shape[0]
    local_blocks = left_factor.shape[0]
    block_size = left_factor.shape[2]
    wide_count = lax.axis_size("wide")
    left_full, right_full = (
        lax.all_gather(left_factor, "dp", axis=1, tiled=True),
        lax.all_gather(right_factor, "dp", axis=1, tiled=True),
    )
    grid = column_map.reshape(block_size, block_size)
    block_order = grid[0] // block_size
    lane_order = grid[:, 0] % block_size
    counting = jnp.arange(block_size, dtype=jnp.int32)
    block_inverse = jnp.zeros((block_size,), jnp.int32).at[block_order].set(counting)
    lane_inverse = jnp.zeros((block_size,), jnp.int32).at[lane_order].set(counting)
    dest_device = jnp.arange(wide_count, dtype=jnp.int32)[:, None, None]
    own_block = jnp.arange(local_blocks, dtype=jnp.int32)[None, :, None]
    dest_block = jnp.arange(local_blocks, dtype=jnp.int32)[None, None, :]
    forward_index = (
        own_block * block_size + lane_order[dest_device * local_blocks + dest_block]
    ).reshape(-1)
    source_block = jnp.arange(local_blocks, dtype=jnp.int32)[:, None]
    target_block = lane_inverse[None, :]
    backward_index = (
        target_block // local_blocks * (local_blocks * local_blocks)
        + source_block * local_blocks
        + target_block % local_blocks
    ).reshape(-1)
    x_blocks = tokens.reshape(row_count, local_blocks, block_size)
    g_blocks = cotangent.reshape(row_count, local_blocks, block_size)
    pre_act = jnp.einsum("tbi,bij->bjt", x_blocks, left_full, preferred_element_type=jnp.float32)
    activated, slope = gelu_parts(pre_act)
    hidden = activated.astype(jnp.bfloat16).reshape(local_blocks * block_size, row_count)
    send_hidden = jnp.take(hidden, forward_index, axis=0).reshape(
        wide_count, local_blocks, local_blocks, row_count
    )
    received = lax.all_to_all(send_hidden, "wide", split_axis=0, concat_axis=0, tiled=True)
    count = received.shape[3]
    flat = received.reshape(wide_count * local_blocks, local_blocks, count)
    mixed = jnp.take(flat, block_order, axis=0)
    grad_right_part = jnp.einsum(
        "rkt,tkj->krj", mixed, g_blocks, preferred_element_type=jnp.float32
    )
    d_mixed = jnp.einsum(
        "tcj,cij->ict", g_blocks, right_full, preferred_element_type=jnp.float32
    ).astype(jnp.bfloat16)
    received = lax.all_to_all(
        jnp.take(d_mixed, block_inverse, axis=0).reshape(
            wide_count, local_blocks, local_blocks, row_count
        ),
        "wide",
        split_axis=0,
        concat_axis=0,
        tiled=True,
    )
    count = received.shape[3]
    flat = received.reshape(wide_count * local_blocks * local_blocks, count)
    d_hidden = jnp.take(flat, backward_index, axis=0).reshape(local_blocks, block_size, count)
    right_share = lax.psum_scatter(grad_right_part, "dp", scatter_dimension=1, tiled=True)
    d_pre = (d_hidden.astype(jnp.float32) * slope).astype(jnp.bfloat16)
    grad_left_part = jnp.einsum("tbi,bjt->bij", x_blocks, d_pre, preferred_element_type=jnp.float32)
    grad_tokens = (
        jnp.einsum("bjt,bij->tbi", d_pre, left_full, preferred_element_type=jnp.float32)
        .astype(jnp.bfloat16)
        .reshape(row_count, local_blocks * block_size)
    )
    left_share = lax.psum_scatter(grad_left_part, "dp", scatter_dimension=1, tiled=True)
    return (grad_tokens, left_share, right_share)


def solution(mesh):
    return jax.shard_map(
        shards,
        mesh=mesh,
        in_specs=(
            P("dp", "wide"),
            P("dp", "wide"),
            P("wide", "dp", None),
            P("wide", "dp", None),
            P(),
        ),
        out_specs=(P("dp", "wide"), P("wide", "dp", None), P("wide", "dp", None)),
        check_vma=False,
    )
```

profile of v0, /device:TPU:0, one launch (start us, length us, event | category | flops | bytes accessed | tf_op | source)
XLA Modules:
  0.0 2076.4 jit_solution(16465413029908930202)
XLA Ops:
  7.2 1.2 compare_and_fusion.1
  8.4 1.0 scatter_custom_fusion
  9.4 0.0 copy-done.7
  9.4 8.8 all_gather.6
  18.3 26.9 %convert_bitcast_fusion = bf16[128,16,8192]{2,0,1:T(8,128)(2,1)} fusion(bf16[16,128,128]{2,1,0:T(8,128)(2,1)S(1)} %all_gather.6, bf16[8192,2048]{1,0:T(8,128)(2,1)} %param.10), kind=kOutput, calls=%fused_computation.26 | convolution fusion | flops 4311744512 | bytes 67633152 | tf_op jit(solution)/shard_map/tcj,cij->ict/dot_general | solution.py:62
  45.1 29.2 %copy.32 = bf16[128,16,8192]{2,1,0:T(8,128)(2,1)} copy(bf16[128,16,8192]{2,0,1:T(8,128)(2,1)} %convert_bitcast_fusion) | data formatting | bytes 67108864 | tf_op jit(solution)/shard_map/convert_element_type | solution.py:64
  74.4 23.0 %gather_fusion.1 = bf16[128,16,8192]{2,1,0:T(8,128)(2,1)} fusion(bf16[128,16,8192]{2,1,0:T(8,128)(2,1)} %copy.32, s32[1024]{0:T(1024)S(1)} %pad_clamp_fusion.2), kind=kCustom, calls=%fused_computation.clone | custom fusion | bytes 67109376 | tf_op jit(solution)/shard_map/jit(_take)/gather | solution.py:66
  97.3 22.8 %broadcast_select_fusion.1 = bf16[128,16,8192]{2,1,0:T(8,128)(2,1)} fusion(bf16[128,16,8192]{2,1,0:T(8,128)(2,1)} %gather_fusion.1, pred[128]{0:T(512)(128)(4,1)S(1)} %compare_and_fusion.2), kind=kLoop, calls=%fused_computation.28 | loop fusion | flops 16777216 | bytes 67108992 | tf_op jit(solution)/shard_map/jit(_take)/select_n | solution.py:66
  120.1 7.2 all-to-all-start
  127.4 0.1 compare_select_fusion.3
  127.5 0.1 reshape.193
  127.6 0.0 copy-done.3
  127.6 0.1 slice_reduce_fusion
  127.7 1.2 gather_fusion
  128.9 0.1 add.159
  129.0 0.1 broadcast_add_fusion
  129.1 0.1 add.162
  129.2 1.0 scatter_custom_fusion.1
  130.2 0.0 copy-done.2
  130.2 7.5 all_gather.7
  137.7 0.1 fusion.30
  137.7 0.1 fusion.27
  137.8 0.6 compare_and_fusion
  138.4 0.6 fusion.31
  139.0 711.5 %all-to-all-done = bf16[8,16,16,8192]{3,2,1,0:T(8,128)(2,1)} async-done(((bf16[8,16,16,8192]{3,2,1,0:T(8,128)(2,1)}), bf16[8,16,16,8192]{3,2,1,0:T(8,128)(2,1)}, u32[]{:S(2)}, u32[]{:S(2)}) %all-to-all-start) | async-done | bytes 33554464 | tf_op jit(solution)/shard_map/all_to_all | solution.py:65
  850.5 106.0 %gather_fusion.2 = bf16[2048,8192]{1,0:T(8,128)(2,1)} fusion(bf16[2048,8192]{1,0:T(8,128)(2,1)} %bitcast.4, s32[2048]{0:T(1024)S(1)} %fusion.27), kind=kCustom, calls=%fused_computation.1.clone | custom fusion | bytes 67117056 | tf_op jit(solution)/shard_map/jit(_take)/gather | solution.py:76
  956.5 22.8 %broadcast_select_fusion.3 = bf16[2048,8192]{1,0:T(8,128)(2,1)} fusion(bf16[2048,8192]{1,0:T(8,128)(2,1)} %gather_fusion.2, pred[2048]{0:T(1024)(128)(4,1)S(1)} %fusion.30), kind=kLoop, calls=%fused_computation.30 | loop fusion | flops 16777216 | bytes 67110912 | tf_op jit(solution)/shard_map/jit(_take)/select_n | solution.py:76
  979.4 0.0 copy-done
  979.4 0.0 copy-start.4
  979.4 58.0 %multiply_convert_fusion = (bf16[16,128,8192]{2,1,0:T(8,128)(2,1)}, bf16[16,128,8192]{2,1,0:T(8,128)(2,1)}) fusion(bf16[16,128,8192]{2,1,0:T(8,128)(2,1)} %bitcast.77, bf16[16,128,128]{2,1,0:T(8,128)(2,1)S(1)} %all_gather.7, bf16[8192,2048]{1,0:T(8,128)(2,1)} %param.9), kind=kOutput, calls=%fused_computation.16 | convolution fusion | flops 4664066048 | bytes 134742016 | tf_op jit(solution)/shard_map/tbi,bij->bjt/dot_general | solution.py:49
  1037.3 0.0 copy-done.4
  1037.4 106.5 %gather_fusion.3 = bf16[2048,8192]{1,0:T(8,128)(2,1)} fusion(bf16[2048,8192]{1,0:T(8,128)(2,1)} %bitcast.73, s32[2048]{0:T(1024)S(1)} %copy-done.4), kind=kCustom, calls=%fused_computation.3.clone | custom fusion | bytes 67117056 | tf_op jit(solution)/shard_map/jit(_take)/gather | solution.py:52
  1143.9 22.8 %broadcast_select_fusion.2 = bf16[2048,8192]{1,0:T(8,128)(2,1)} fusion(bf16[2048,8192]{1,0:T(8,128)(2,1)} %gather_fusion.3, pred[2048]{0:T(1024)(128)(4,1)S(1)} %copy-done.5), kind=kLoop, calls=%fused_computation.29 | loop fusion | flops 16777216 | bytes 67110912 | tf_op jit(solution)/shard_map/jit(_take)/select_n | solution.py:52
  1166.7 7.2 all-to-all-start.1
  1173.9 0.0 reduce-scatter.3.cloned.1.call-start
  1174.0 22.8 %fusion.22 = f32[16,128,128]{1,2,0:T(8,128)S(1)} fusion(bf16[16,128,8192]{2,1,0:T(8,128)(2,1)} %get-tuple-element.22, bf16[8192,2048]{1,0:T(8,128)(2,1)} %param.9), kind=kOutput, calls=%fused_computation.36 | convolution fusion | flops 4294967296 | bytes 68157440 | tf_op jit(solution)/shard_map/tbi,bjt->bij/dot_general | solution.py:79
  1196.8 1.4 copy.35
  1198.2 0.0 reduce-scatter.3.cloned.1.call-update
  1198.2 0.0 reduce-scatter.5.cloned.1.call-start
  1198.3 698.0 %all-to-all-done.1 = bf16[8,16,16,8192]{3,2,1,0:T(8,128)(2,1)} async-done(((bf16[8,16,16,8192]{3,2,1,0:T(8,128)(2,1)}), bf16[8,16,16,8192]{3,2,1,0:T(8,128)(2,1)}, u32[]{:S(2)}, u32[]{:S(2)}) %all-to-all-start.1) | async-done | bytes 33554464 | tf_op jit(solution)/shard_map/all_to_all | solution.py:55
  1896.3 23.0 %gather_fusion.4 = bf16[128,16,8192]{2,1,0:T(8,128)(2,1)} fusion(bf16[128,16,8192]{2,1,0:T(8,128)(2,1)} %bitcast.11, s32[1024]{0:T(1024)S(1)} %pad_clamp_fusion), kind=kCustom, calls=%fused_computation.2.clone | custom fusion | bytes 67109376 | tf_op jit(solution)/shard_map/jit(_take)/gather | solution.py:58
  1919.2 0.0 copy-done.6
  1919.2 22.8 %broadcast_select_fusion = bf16[128,16,8192]{2,1,0:T(8,128)(2,1)} fusion(bf16[128,16,8192]{2,1,0:T(8,128)(2,1)} %gather_fusion.4, pred[128]{0:T(512)(128)(4,1)S(1)} %copy-done.6), kind=kLoop, calls=%fused_computation.27 | loop fusion | flops 16777216 | bytes 67108992 | tf_op jit(solution)/shard_map/jit(_take)/select_n | solution.py:58
  1942.1 57.8 %fusion.11 = f32[16,128,128]{2,1,0:T(8,128)} fusion(bf16[128,16,8192]{2,1,0:T(8,128)(2,1)} %broadcast_select_fusion, bf16[8192,2048]{1,0:T(8,128)(2,1)} %param.10), kind=kOutput, calls=%fused_computation.21 | convolution fusion | flops 4294967296 | bytes 68157440 | tf_op jit(solution)/shard_map/rkt,tkj->krj/dot_general | solution.py:59
  1999.9 0.0 reduce-scatter.5.cloned.1.call-update
  1999.9 23.2 %convolution_convert_fusion = bf16[16,8192,128]{1,2,0:T(8,128)(2,1)} fusion(bf16[16,128,128]{2,1,0:T(8,128)(2,1)S(1)} %copy-done.1, bf16[16,128,8192]{2,1,0:T(8,128)(2,1)} %get-tuple-element.22), kind=kOutput, calls=%fused_computation.35 | convolution fusion | flops 4311744512 | bytes 67633152 | tf_op jit(solution)/shard_map/bjt,bij->tbi/dot_general | solution.py:81
  2023.1 44.3 %copy.38 = bf16[8192,2048]{1,0:T(8,128)(2,1)} copy(bf16[8192,2048]{0,1:T(8,128)(2,1)} %bitcast.76) | data formatting | bytes 67108864
  2067.3 1.7 copy.39
  (25 shorter events, 0.1 us)
Async XLA Ops:
  8.4 1.0 copy-start.7
  120.1 7.4 copy-start.3
  120.1 10.0 copy-start.2
  120.1 730.4 %all-to-all-start = ((bf16[8,16,16,8192]{3,2,1,0:T(8,128)(2,1)}), bf16[8,16,16,8192]{3,2,1,0:T(8,128)(2,1)}, u32[]{:S(2)}, u32[]{:S(2)}) async-start(bf16[8,16,16,8192]{3,2,1,0:T(8,128)(2,1)} %bitcast.74), calls=%async_computation | async-start | bytes 67108864 | tf_op jit(solution)/shard_map/all_to_all | solution.py:65
  137.6 841.7 %copy-start = (bf16[16,128,128]{2,1,0:T(8,128)(2,1)}, bf16[16,128,128]{2,1,0:T(8,128)(2,1)S(1)}, u32[]{:S(2)}) copy-start(bf16[16,128,128]{2,1,0:T(8,128)(2,1)S(1)} %all_gather.7) | copy-start | bytes 1572868
  979.4 58.0 %copy-start.4 = (s32[2048]{0:T(1024)S(1)}, s32[2048]{0:T(1024)}, u32[]{:S(2)}) copy-start(s32[2048]{0:T(1024)} %fusion.31) | copy-start | bytes 24580
  1037.3 106.5 %copy-start.5 = (pred[2048]{0:T(1024)(128)(4,1)S(1)}, pred[2048]{0:T(1024)(128)(4,1)}, u32[]{:S(2)}) copy-start(pred[2048]{0:T(1024)(128)(4,1)} %compare_and_fusion) | copy-start | bytes 6148
  1166.7 7.3 copy-start.8
  1166.7 729.6 %all-to-all-start.1 = ((bf16[8,16,16,8192]{3,2,1,0:T(8,128)(2,1)}), bf16[8,16,16,8192]{3,2,1,0:T(8,128)(2,1)}, u32[]{:S(2)}, u32[]{:S(2)}) async-start(bf16[8,16,16,8192]{3,2,1,0:T(8,128)(2,1)} %bitcast.75), calls=%async_computation.2 | async-start | bytes 67108864 | tf_op jit(solution)/shard_map/all_to_all | solution.py:55
  1173.9 893.4 %reduce-scatter.3.cloned.1.call-start = ((), (), s32[]{:S(2)}) async-start(), calls=%async_computation.4 | async-start | bytes 1310720 | tf_op jit(solution)/shard_map/reduce_scatter | solution.py:85
  1198.2 870.9 %reduce-scatter.5.cloned.1.call-start = ((), (), s32[]{:S(2)}) async-start(), calls=%async_computation.5 | async-start | bytes 1310720 | tf_op jit(solution)/shard_map/reduce_scatter | solution.py:77
  1896.3 23.0 %copy-start.6 = (pred[128]{0:T(512)(128)(4,1)S(1)}, pred[128]{0:T(512)(128)(4,1)}, u32[]{:S(2)}) copy-start(pred[128]{0:T(512)(128)(4,1)} %get-tuple-element.19) | copy-start | bytes 388
  1942.1 57.8 %copy-start.1 = (bf16[16,128,128]{2,1,0:T(8,128)(2,1)S(1)}, bf16[16,128,128]{2,1,0:T(8,128)(2,1)}, u32[]{:S(2)}) copy-start(bf16[16,128,128]{2,1,0:T(8,128)(2,1)} %copy-done) | copy-start | bytes 1572868
Sparse Core Ops, SparseCore 0:
  1198.3 25.7 reduce-scatter.2
  2000.0 23.5 reduce-scatter.4
where the time goes:
time: 2090 us; the launch traced here: 2080 us
  waiting for transfers between devices  1410 us (67%)
  local copies, waits for them, and re-layouts  339 us (16%)
  matrix products  189 us (9%)
  other arithmetic  94.2 us (5%)
    all_to_all x1, waiting for transfers between devices, shards(): lax.all_to_all(jnp.take(d_mixed, block_inverse, axis=0).reshape(wide_coun...  712 us
    all_to_all x1, waiting for transfers between devices, shards(): lax.all_to_all(send_hidden, 'wide', split_axis=0, concat_axis=0, tiled=True)  698 us
    gather x1, local copies, waits for them, and re-layouts, shards(): jnp.take(hidden, forward_index, axis=0)  107 us
    gather x1, local copies, waits for them, and re-layouts, shards(): jnp.take(flat, backward_index, axis=0)  106 us
    dot_general x1, matrix products, shards(): jnp.einsum('tbi,bij->bjt', x_blocks, left_full, preferred_element_type=jn...  58 us
    dot_general x1, matrix products, shards(): jnp.einsum('rkt,tkj->krj', mixed, g_blocks, preferred_element_type=jnp.fl...  57.8 us
    unnamed x20, local copies, waits for them, and re-layouts  46 us
  transfers between devices with their start and end apart: 4, of which 2 were waited for; matrix products, arithmetic and copies ran while one was open for 10% of the time, Pallas kernels for 0%

commit v1 on v0

v1 whole, which is shorter than its diff:
```python
import functools

import jax
import jax.numpy as jnp
from jax import lax
from jax.experimental import pallas as pl
from jax.experimental.pallas import tpu as pltpu
from jax.sharding import PartitionSpec as P

gelu_scale = 0.7978845608
gelu_cubic = 0.044715
f32 = jnp.float32
bf16 = jnp.bfloat16
lane_count = 128


def gelu_tanh(value):
    return jnp.tanh(gelu_scale * (value + gelu_cubic * value * value * value))


def gelu_value(value):
    return 0.5 * value * (1.0 + gelu_tanh(value))


def gelu_slope(value):
    tanh_part = gelu_tanh(value)
    return 0.5 * (1.0 + tanh_part) + 0.5 * value * (1.0 - tanh_part * tanh_part) * gelu_scale * (
        1.0 + 3.0 * gelu_cubic * value * value
    )


def dot(a, b, a_dim, b_dim, precision=None):
    return lax.dot_general(
        a, b, (((a_dim,), (b_dim,)), ((), ())), precision=precision, preferred_element_type=f32
    )


def params(steps):
    return pltpu.CompilerParams(
        dimension_semantics=("arbitrary",) * steps, vmem_limit_bytes=48 * 1024 * 1024
    )


def cost(flops, bytes_accessed, transcendentals=0):
    return pl.CostEstimate(
        flops=int(flops), bytes_accessed=int(bytes_accessed), transcendentals=int(transcendentals)
    )


def after(value, earlier):
    return value if earlier is None else lax.optimization_barrier((value, earlier))[0]


def exchange(send):
    return lax.all_to_all(send, "wide", split_axis=0, concat_axis=0, tiled=True)


def cuts(total, weights, unit=1):
    edges, done = [0], 0
    for weight in weights:
        done += weight
        edges.append(total * done // sum(weights) // unit * unit)
    return [(a, b) for a, b in zip(edges[:-1], edges[1:]) if b > a]


def right_sent_kernel(map_ref, factor_ref, out_ref):
    size = factor_ref.shape[1]
    order = map_ref[0:1, :] // size
    pick = jnp.where(lax.broadcasted_iota(jnp.int32, (size, size), 0) == order, 1.0, 0.0).astype(bf16)
    for c in range(factor_ref.shape[0]):
        out_ref[c] = dot(pick, factor_ref[c], 1, 0).astype(bf16)


def left_sent_kernel(map_ref, factor_ref, out_ref):
    size = factor_ref.shape[1]
    order = map_ref[:, 0:1] % size
    pick = jnp.where(lax.broadcasted_iota(jnp.int32, (size, size), 1) == order, 1.0, 0.0).astype(bf16)
    for b in range(factor_ref.shape[0]):
        out_ref[b] = dot(pick, factor_ref[b], 1, 1).astype(bf16)


def left_done_kernel(map_ref, total_ref, *refs):
    out_refs, rows_ref = refs[:-1], refs[-1]
    size = total_ref.shape[1]
    order = map_ref[:, 0:1] % size
    pick = jnp.where(lax.broadcasted_iota(jnp.int32, (size, size), 1) == order, 1.0, 0.0)
    for b in range(total_ref.shape[0]):
        rows_ref[...] = dot(total_ref[b], pick, 0, 0, lax.Precision.HIGHEST)
        share_out(rows_ref, out_refs, b)


def share_out(rows_ref, out_refs, at):
    rows = rows_ref.shape[0] // len(out_refs)
    own = lax.axis_index("dp")
    for s, out_ref in enumerate(out_refs):
        out_ref[at] = rows_ref[pl.ds(pl.multiple_of((own ^ s) * rows, rows), rows), :]


def left_done(grid_map, total):
    dp = lax.axis_size("dp")
    blocks, size, _ = total.shape
    return pl.pallas_call(
        left_done_kernel,
        out_shape=[jax.ShapeDtypeStruct((blocks, size // dp, size), f32)] * dp,
        scratch_shapes=[pltpu.VMEM((size, size), f32)],
        cost_estimate=cost(12 * total.size * size, 8 * total.size),
        compiler_params=params(0),
    )(grid_map, total)


def ordered(kernel, grid_map, factor):
    return pl.pallas_call(
        kernel,
        out_shape=jax.ShapeDtypeStruct(factor.shape, bf16),
        cost_estimate=cost(2 * factor.size * factor.shape[2], 4 * factor.size),
        compiler_params=params(0),
    )(grid_map, factor)


def send_kernel(activate, x_ref, w_ref, out_ref, wide_ref):
    blocks, size = w_ref.shape[0], w_ref.shape[-1]
    dests, count = w_ref.shape[1], w_ref.shape[2]
    width = dests * count
    pieces = wide_ref.shape[0]
    pitch = wide_ref.shape[1] // blocks
    for p in range(blocks):
        factor = w_ref[p].reshape(width, size)
        y = dot(factor, x_ref[:, p * size : (p + 1) * size], 1, 1)
        if activate:
            y = gelu_value(y)
        for k in range(pieces):
            wide_ref[k, p * pitch : p * pitch + width, :] = y[:, k * lane_count : (k + 1) * lane_count]
    for dest in range(dests):
        for n in range(count):
            for k in range(pieces):
                rows = wide_ref[k, pl.ds(dest * count + n, blocks, stride=pitch), :]
                out_ref[dest, n, :, k * lane_count : (k + 1) * lane_count] = rows.astype(bf16)


def send_part(x, factor, rows, part, activate, tile):
    blocks, wide, _, size = factor.shape
    (start, stop), (first, last) = rows, part
    count, length = last - first, stop - start
    width = wide * count
    taken = factor[:, :, first:last]
    pitch = -(-width // 8) * 8 + 8
    return pl.pallas_call(
        functools.partial(send_kernel, activate),
        grid=(length // tile,),
        in_specs=[
            pl.BlockSpec((tile, blocks * size), lambda i: (start // tile + i, 0)),
            pl.BlockSpec((blocks, wide, count, size), lambda i: (0, 0, 0, 0)),
        ],
        out_specs=pl.BlockSpec((wide, count, blocks, tile), lambda i: (0, 0, 0, i)),
        out_shape=jax.ShapeDtypeStruct((wide, count, blocks, length), bf16),
        scratch_shapes=[pltpu.VMEM((tile // lane_count, blocks * pitch, lane_count), f32)],
        cost_estimate=cost(
            2 * length * blocks * width * size,
            2 * length * blocks * (size + width),
            length * blocks * width if activate else 0,
        ),
        compiler_params=params(1),
    )(x, taken)


def right_kernel(map_ref, received_ref, g_ref, *refs):
    out_refs, rows_ref = refs[:-1], refs[-1]
    size = g_ref.shape[1]
    total = dot(received_ref[:, 0].reshape(size, received_ref.shape[3]), g_ref[...], 1, 0)
    order = map_ref[0:1, :] // size
    pick = jnp.where(lax.broadcasted_iota(jnp.int32, (size, size), 0) == order, 1.0, 0.0)
    rows_ref[...] = dot(pick, total, 0, 0, lax.Precision.HIGHEST)
    share_out(rows_ref, out_refs, 0)


def right_part(grid_map, received, cotangent, part, first):
    dp = lax.axis_size("dp")
    wide, _, blocks, length = received.shape
    size = grid_map.shape[0]
    count, skip = part[1] - part[0], part[0] - first
    return pl.pallas_call(
        right_kernel,
        grid=(count,),
        in_specs=[
            pl.BlockSpec((size, size), lambda n: (0, 0)),
            pl.BlockSpec((wide, 1, blocks, length), lambda n: (0, skip + n, 0, 0)),
            pl.BlockSpec((length, size), lambda n: (0, part[0] + n)),
        ],
        out_specs=[pl.BlockSpec((1, size // dp, size), lambda n: (n, 0, 0))] * dp,
        out_shape=[jax.ShapeDtypeStruct((count, size // dp, size), f32)] * dp,
        scratch_shapes=[pltpu.VMEM((size, size), f32)],
        cost_estimate=cost(2 * count * size * size * length, 4 * count * size * length),
        compiler_params=params(1),
    )(grid_map, received, cotangent)


def back_kernel(has_total, received_ref, x_ref, w_ref, *refs):
    if has_total:
        _, earlier_ref, rows_ref, total_ref = refs
    else:
        rows_ref, total_ref = refs
    blocks, size = w_ref.shape[0], w_ref.shape[1]
    tile = x_ref.shape[0]

    @pl.when(pl.program_id(0) == 0)
    def _():
        if has_total:
            total_ref[...] = earlier_ref[...]
        else:
            total_ref[...] = jnp.zeros_like(total_ref)

    for b in range(blocks):
        x = x_ref[:, b * size : (b + 1) * size]
        slope = gelu_slope(dot(w_ref[b], x, 1, 1))
        d_hidden = received_ref[:, b].reshape(size, tile).astype(f32)
        d_pre = (d_hidden * slope).astype(bf16)
        total_ref[b] += dot(d_pre, x, 1, 0)
        rows_ref[:, b * size : (b + 1) * size] = dot(d_pre, w_ref[b], 0, 0).astype(bf16)


def back_part(received, tokens, factor, rows, earlier, tile):
    wide, blocks, _, length = received.shape
    size = factor.shape[1]
    start = rows[0] // tile
    whole_factor = pl.BlockSpec((blocks, size, size), lambda i: (0, 0, 0))
    in_specs = [
        pl.BlockSpec((wide, blocks, blocks, tile), lambda i: (0, 0, 0, i)),
        pl.BlockSpec((tile, blocks * size), lambda i: (start + i, 0)),
        whole_factor,
    ]
    operands = [received, tokens, factor]
    aliases = {}
    if earlier is not None:
        in_specs += [pl.BlockSpec(memory_space=pl.ANY), whole_factor]
        operands += list(earlier)
        aliases = {3: 0}
    return pl.pallas_call(
        functools.partial(back_kernel, earlier is not None),
        grid=(length // tile,),
        in_specs=in_specs,
        out_specs=[pl.BlockSpec((tile, blocks * size), lambda i: (start + i, 0)), whole_factor],
        out_shape=[
            jax.ShapeDtypeStruct(tokens.shape, bf16),
            jax.ShapeDtypeStruct((blocks, size, size), f32),
        ],
        input_output_aliases=aliases,
        cost_estimate=cost(
            6 * length * blocks * size * size, 6 * length * blocks * size, length * blocks * size
        ),
        compiler_params=params(1),
    )(*operands)


def sum_over_dp(pieces):
    total = pieces[0]
    for s in range(1, len(pieces)):
        total = total + lax.ppermute(pieces[s], "dp", [(i, i ^ s) for i in range(len(pieces))])
    return total


def with_kernels(tokens, cotangent, left_factor, right_factor, column_map):
    row_count = tokens.shape[0]
    blocks = left_factor.shape[0]
    size = left_factor.shape[2]
    wide = lax.axis_size("wide")
    tile = 512

    grid_map = column_map.reshape(size, size)
    right_full = lax.all_gather(right_factor, "dp", axis=1, tiled=True)
    right_sent = ordered(right_sent_kernel, grid_map, right_full)
    left_full = lax.all_gather(left_factor, "dp", axis=1, tiled=True)
    left_sent = ordered(left_sent_kernel, grid_map, left_full)
    by_dest = (blocks, wide, blocks, size)
    everything = (0, row_count)

    row_cuts = cuts(row_count, row_weights, tile)
    block_cuts = cuts(blocks, block_weights)
    last, arrived = None, []
    for rows in row_cuts:
        send = send_part(cotangent, right_sent.reshape(by_dest), rows, (0, blocks), False, tile)
        last = exchange(after(send, last))
        arrived.append(last)

    received = []
    for part in block_cuts[:-1]:
        send = send_part(tokens, left_sent.reshape(by_dest), everything, part, True, tile)
        last = exchange(after(send, last))
        received.append(last)

    earlier = None
    for rows, got in zip(row_cuts, arrived):
        earlier = back_part(got, tokens, left_sent, rows, earlier, tile)
    grad_tokens, left_total = earlier
    left_share = sum_over_dp(left_done(grid_map, left_total))

    part = block_cuts[-1]
    send = send_part(tokens, left_sent.reshape(by_dest), everything, part, True, tile)
    last = exchange(after(send, (last, left_share)))

    shares = []
    for (first, stop), got in zip(block_cuts, received):
        half = (first + stop) // 2
        for piece in ((first, half), (half, stop)):
            if piece[1] > piece[0]:
                shares.append(sum_over_dp(right_part(grid_map, got, cotangent, piece, first)))
    shares.append(sum_over_dp(right_part(grid_map, last, cotangent, part, part[0])))
    return (grad_tokens, left_share, jnp.concatenate(shares, axis=0))


row_weights = (1, 15)
block_weights = (15, 1)


def plain(tokens, cotangent, left_factor, right_factor, column_map):
    row_count = tokens.shape[0]
    blocks = left_factor.shape[0]
    size = left_factor.shape[2]
    wide = lax.axis_size("wide")

    grid = column_map.reshape(size, size)
    block_order = grid[0] // size
    lane_order = grid[:, 0] % size
    counting = jnp.arange(size, dtype=jnp.int32)
    lane_pick = (lane_order[:, None] == counting[None, :]).astype(bf16)
    block_pick = (block_order[None, :] == counting[:, None]).astype(bf16)
    lane_inverse = jnp.sum(jnp.where(lane_order[None, :] == counting[:, None], counting[None, :], 0), axis=1)

    right_full = lax.all_gather(right_factor, "dp", axis=1, tiled=True)
    left_full = lax.all_gather(left_factor, "dp", axis=1, tiled=True)
    left_sent = jnp.einsum("cl,bil->bci", lane_pick, left_full, preferred_element_type=f32).astype(bf16)
    right_sent = jnp.einsum("br,crj->cbj", block_pick, right_full, preferred_element_type=f32).astype(bf16)

    x_blocks = tokens.reshape(row_count, blocks, size)
    g_blocks = cotangent.reshape(row_count, blocks, size)

    d_mixed = jnp.einsum("tcj,cbj->cbt", g_blocks, right_sent, preferred_element_type=f32)
    d_mixed = d_mixed.astype(bf16).reshape(blocks, wide, blocks, row_count)
    arrived = exchange(d_mixed.transpose(1, 2, 0, 3))

    pre_act = jnp.einsum("tbi,bci->bct", x_blocks, left_sent, preferred_element_type=f32)
    hidden = gelu_value(pre_act).astype(bf16).reshape(blocks, wide, blocks, row_count)
    received = exchange(after(hidden.transpose(1, 2, 0, 3), arrived))

    d_hidden = arrived.transpose(1, 0, 2, 3).reshape(blocks, size, row_count)
    d_pre = (d_hidden.astype(f32) * gelu_slope(pre_act)).astype(bf16)
    left_total = jnp.einsum("bct,tbi->bic", d_pre, x_blocks, preferred_element_type=f32)
    grad_tokens = jnp.einsum("bct,bci->tbi", d_pre, left_sent, preferred_element_type=f32)
    left_share = lax.psum_scatter(left_total, "dp", scatter_dimension=1, tiled=True)
    left_share = jnp.take(left_share, lane_inverse, axis=2)

    right_total = jnp.einsum("snbt,tnj->nsbj", received, g_blocks, preferred_element_type=f32)
    right_total = jnp.take(right_total.reshape(blocks, size, size), block_order, axis=1)
    right_share = lax.psum_scatter(right_total, "dp", scatter_dimension=1, tiled=True)
    return (grad_tokens.astype(bf16).reshape(row_count, blocks * size), left_share, right_share)


def shards(*args):
    blocks, size = args[2].shape[0], args[2].shape[2]
    dp = lax.axis_size("dp")
    fits = blocks % 16 == 0 and size == lane_count and dp & (dp - 1) == 0 and size % (8 * dp) == 0
    return (with_kernels if fits else plain)(*args)


def solution(mesh):
    return jax.shard_map(
        shards,
        mesh=mesh,
        in_specs=(
            P("dp", "wide"),
            P("dp", "wide"),
            P("wide", "dp", None),
            P("wide", "dp", None),
            P(),
        ),
        out_specs=(P("dp", "wide"), P("wide", "dp", None), P("wide", "dp", None)),
        check_vma=False,
    )
```

time: 2090 us -> 1500 us (0.72)
  local copies, waits for them, and re-layouts: 339 us -> 2.25 us
  Pallas kernels: 0 us -> 267 us
  waiting for transfers between devices: 1410 us -> 1180 us
  matrix products: 189 us -> 0 us
  other arithmetic: 94.2 us -> 1.58 us
    pallas_call x0 -> x12, Pallas kernels: none -> 267 us  [the longest x4 139 us: send_part(): pl.pallas_call(functools.partial(send_kernel, activate), grid=(length //...]
    gather x5 -> x0, local copies, waits for them, and re-layouts: 260 us -> none  [the longest x1 107 us: shards(): jnp.take(hidden, forward_index, axis=0)]
    all_to_all x2 -> x4, waiting for transfers between devices: 1410 us -> 1180 us  [exchange(): return lax.all_to_all(send, 'wide', split_axis=0, concat_axis=0, tiled=True)]
    dot_general x5 -> x0, matrix products: 189 us -> none  [the longest x1 58 us: shards(): jnp.einsum('tbi,bij->bjt', x_blocks, left_full, preferred_element_type=jn...]
    select_n x7 -> x0, other arithmetic: 91.4 us -> none  [the longest x2 22.8 us: shards(): jnp.take(d_mixed, block_inverse, axis=0)]
    unnamed x20 -> x8, local copies, waits for them, and re-layouts: 46 us -> 2.18 us
    convert_element_type x1 -> x0, local copies, waits for them, and re-layouts: 29.2 us -> none  [shards(): d_mixed = jnp.einsum('tcj,cij->ict', g_blocks, right_full, preferred_elem...]
  transfers between devices with their start and end apart: 4 -> 16, of which waited for: 2 -> 6; matrix products, arithmetic and copies ran while one was open for 10% -> 0% of each run, Pallas kernels for 0% -> 18%
where the time goes in v1:
time: 1500 us
  waiting for transfers between devices  1180 us (79%)
  Pallas kernels  267 us (18%)
  starting transfers between devices  31.8 us (2%)
  blocking collectives  15.6 us (1%)
    all_to_all x4, waiting for transfers between devices, exchange(): return lax.all_to_all(send, 'wide', split_axis=0, concat_axis=0, tiled=True)  1180 us
    pallas_call x4, Pallas kernels, send_part(): pl.pallas_call(functools.partial(send_kernel, activate), grid=(length //...  139 us
    pallas_call x2, Pallas kernels, back_part(): pl.pallas_call(functools.partial(back_kernel, earlier is not None), grid=...  96 us
    pallas_call x3, Pallas kernels, right_part(): pl.pallas_call(right_kernel, grid=(count,), in_specs=[pl.BlockSpec((size,...  30.4 us
  transfers between devices with their start and end apart: 16, of which 6 were waited for; matrix products, arithmetic and copies ran while one was open for 0% of the time, Pallas kernels for 18%

profile of v1, /device:TPU:0, one launch (start us, length us, event | category | flops | bytes accessed | tf_op | source)
XLA Modules:
  0.0 1496.7 jit_solution(5620110580859221753)
XLA Ops:
  0.6 8.8 all_gather.6.factor_ref
  9.5 0.8 copy-done.1
  10.3 0.3 shard_map.76
  10.6 3.2 shard_map.78
  13.8 1.3 copy-done
  15.1 5.8 all-to-all-start
  20.9 32.4 %shard_map.77 = bf16[8,16,16,7680]{3,2,1,0:T(8,128)(2,1)} custom-call(bf16[8192,2048]{1,0:T(8,128)(2,1)} %g_ref.5, bf16[16,8,16,128]{3,2,1,0:T(8,128)(2,1)S(1)} %bitcast.7), custom_call_target="tpu_custom_call" | custom-call | flops 4026531840 | bytes 62914560 | tf_op jit(solution)/shard_map/pallas_call | solution.py:147
  53.4 16.3 %all-to-all-done.received_ref = bf16[8,16,16,512]{3,2,1,0:T(8,128)(2,1)S(1)} async-done(((bf16[8,16,16,512]{3,2,1,0:T(8,128)(2,1)}), bf16[8,16,16,512]{3,2,1,0:T(8,128)(2,1)S(1)}, u32[]{:S(2)}, u32[]{:S(2)}) %all-to-all-start) | async-done | bytes 2097184 | tf_op jit(solution)/shard_map/all_to_all | solution.py:55
  69.7 6.9 all-to-all-start.1
  76.6 6.8 all_gather.7.factor_ref
  83.4 0.5 shard_map.79.w_ref
  83.9 82.1 %shard_map.83 = bf16[8,15,16,8192]{3,2,1,0:T(8,128)(2,1)} custom-call(bf16[8192,2048]{1,0:T(8,128)(2,1)} %x_ref.11, bf16[16,8,15,128]{3,2,1,0:T(8,128)(2,1)S(1)} %bitcast.4), custom_call_target="tpu_custom_call" | custom-call | flops 4026531840 | bytes 65011712 | tf_op jit(solution)/shard_map/pallas_call | solution.py:147
  166.1 587.6 %all-to-all-done.1.received_ref = bf16[8,16,16,7680]{3,2,1,0:T(8,128)(2,1)} async-done(((bf16[8,16,16,7680]{3,2,1,0:T(8,128)(2,1)}), bf16[8,16,16,7680]{3,2,1,0:T(8,128)(2,1)}, u32[]{:S(2)}, u32[]{:S(2)}) %all-to-all-start.1) | async-done | bytes 31457312 | tf_op jit(solution)/shard_map/all_to_all | solution.py:55
  753.7 7.1 all-to-all-start.2
  760.8 8.4 shard_map.80
  769.2 87.6 %shard_map.81 = (bf16[8192,2048]{1,0:T(8,128)(2,1)}, f32[16,128,128]{2,1,0:T(8,128)S(1)}) custom-call(bf16[8,16,16,7680]{3,2,1,0:T(8,128)(2,1)} %all-to-all-done.1.received_ref, bf16[8192,2048]{1,0:T(8,128)(2,1)} %x_ref.11, bf16[16,128,128]{2,1,0:T(8,128)(2,1)S(1)} %shard_map.79.w_ref, ...), custom_call_target="tpu_custom_call", output_to_operand_aliasing={{0}: (3, {})} | custom-call | flops 12079595520 | bytes 94371840 | tf_op jit(solution)/shard_map/pallas_call | solution.py:237
  856.8 1.2 shard_map.82
  858.0 0.1 collective-permute-start.2
  858.1 1.2 collective-permute-start.1
  859.2 0.7 collective-permute-start
  859.9 0.1 slice.9.w_ref
  860.0 21.3 %shard_map.86 = bf16[8,1,16,8192]{3,2,1,0:T(8,128)(2,1)} custom-call(bf16[8192,2048]{1,0:T(8,128)(2,1)} %x_ref.11, bf16[16,8,1,128]{3,2,1,0:T(2,128)(2,1)S(1)} %slice.9.w_ref), custom_call_target="tpu_custom_call" | custom-call | flops 268435456 | bytes 35651584 | tf_op jit(solution)/shard_map/pallas_call | solution.py:147
  881.3 0.0 collective-permute-done.2
  881.4 0.8 add_add_fusion
  882.1 554.7 %all-to-all-done.2.received_ref = bf16[8,15,16,8192]{3,2,1,0:T(8,128)(2,1)} async-done(((bf16[8,15,16,8192]{3,2,1,0:T(8,128)(2,1)}), bf16[8,15,16,8192]{3,2,1,0:T(8,128)(2,1)}, u32[]{:S(2)}, u32[]{:S(2)}) %all-to-all-start.2) | async-done | bytes 31457312 | tf_op jit(solution)/shard_map/all_to_all | solution.py:55
  1436.8 4.2 all-to-all-start.3
  1441.1 13.1 shard_map.84
  1454.2 0.5 collective-permute-start.5
  1454.7 0.9 collective-permute-start.4
  1455.6 0.5 collective-permute-start.3
  1456.1 14.7 shard_map.85
  1470.8 0.8 collective-permute-start.8
  1471.6 0.9 collective-permute-start.7
  1472.5 0.0 collective-permute-done.5
  1472.5 0.2 collective-permute-start.6
  1472.8 0.0 collective-permute-done.4
  1472.8 0.0 collective-permute-done.3
  1472.8 16.7 %all-to-all-done.3.received_ref = bf16[8,1,16,8192]{3,2,1,0:T(8,128)(2,1)S(1)} async-done(((bf16[8,1,16,8192]{3,2,1,0:T(8,128)(2,1)}), bf16[8,1,16,8192]{3,2,1,0:T(8,128)(2,1)S(1)}, u32[]{:S(2)}, u32[]{:S(2)}) %all-to-all-start.3) | async-done | bytes 2097184 | tf_op jit(solution)/shard_map/all_to_all | solution.py:55
  1489.5 2.5 shard_map.87
  1492.0 0.1 collective-permute-start.11
  1492.1 1.1 collective-permute-start.10
  1493.3 0.0 collective-permute-done.8
  1493.3 0.7 collective-permute-start.9
  1494.0 0.0 collective-permute-done.6
  1494.0 1.3 collective-permute-done.11
  1495.3 0.7 collective-permute-done.10
  1496.0 0.0 collective-permute-done.9
  1496.0 0.7 pad_maximum_fusion
  (12 shorter events, 0.1 us)
Async XLA Ops:
  9.5 0.8 copy-start.1
  13.8 1.3 copy-start
  15.1 54.6 %all-to-all-start = ((bf16[8,16,16,512]{3,2,1,0:T(8,128)(2,1)}), bf16[8,16,16,512]{3,2,1,0:T(8,128)(2,1)S(1)}, u32[]{:S(2)}, u32[]{:S(2)}) async-start(bf16[8,16,16,512]{3,2,1,0:T(8,128)(2,1)} %copy-done), calls=%async_computation | async-start | bytes 4194304 | tf_op jit(solution)/shard_map/all_to_all | solution.py:55
  53.4 23.3 %copy-start.3 = (bf16[16,32,128]{2,1,0:T(8,128)(2,1)S(1)}, bf16[16,32,128]{2,1,0:T(8,128)(2,1)}, u32[]{:S(2)}) copy-start(bf16[16,32,128]{2,1,0:T(8,128)(2,1)} %param.7) | copy-start | bytes 393220
  53.4 30.0 %copy-start.2 = (s32[16384]{0:T(1024)S(1)}, s32[16384]{0:T(1024)}, u32[]{:S(2)}) copy-start(s32[16384]{0:T(1024)} %param.9) | copy-start | bytes 196612
  69.7 684.0 %all-to-all-start.1 = ((bf16[8,16,16,7680]{3,2,1,0:T(8,128)(2,1)}), bf16[8,16,16,7680]{3,2,1,0:T(8,128)(2,1)}, u32[]{:S(2)}, u32[]{:S(2)}) async-start(bf16[8,16,16,7680]{3,2,1,0:T(8,128)(2,1)} %shard_map.77), calls=%async_computation.1 | async-start | bytes 62914560 | tf_op jit(solution)/shard_map/all_to_all | solution.py:55
  753.7 683.1 %all-to-all-start.2 = ((bf16[8,15,16,8192]{3,2,1,0:T(8,128)(2,1)}), bf16[8,15,16,8192]{3,2,1,0:T(8,128)(2,1)}, u32[]{:S(2)}, u32[]{:S(2)}) async-start(bf16[8,15,16,8192]{3,2,1,0:T(8,128)(2,1)} %shard_map.83), calls=%async_computation.2 | async-start | bytes 62914560 | tf_op jit(solution)/shard_map/all_to_all | solution.py:55
  858.0 23.4 %collective-permute-start.2 = (f32[16,32,128]{2,1,0:T(8,128)S(1)}, f32[16,32,128]{2,1,0:T(8,128)S(1)}, u32[]{:S(2)}, u32[]{:S(2)}) collective-permute-start(f32[16,32,128]{2,1,0:T(8,128)S(1)} %get-tuple-element.34), channel_id=1, source_target_pairs={{0,24},{8,16},{16,8},{24,0},{1,25},{9,17},{17,9},{25,1},{2,26},{10... | collective-permute-start | bytes 786440 | tf_op jit(solution)/shard_map/ppermute | solution.py:257
  858.1 23.3 %collective-permute-start.1 = (f32[16,32,128]{2,1,0:T(8,128)S(1)}, f32[16,32,128]{2,1,0:T(8,128)S(1)}, u32[]{:S(2)}, u32[]{:S(2)}) collective-permute-start(f32[16,32,128]{2,1,0:T(8,128)S(1)} %get-tuple-element.33), channel_id=1, source_target_pairs={{0,16},{8,24},{16,0},{24,8},{1,17},{9,25},{17,1},{25,9},{2,18},{10... | collective-permute-start | bytes 786440 | tf_op jit(solution)/shard_map/ppermute | solution.py:257
  859.2 22.1 %collective-permute-start = (f32[16,32,128]{2,1,0:T(8,128)S(1)}, f32[16,32,128]{2,1,0:T(8,128)S(1)}, u32[]{:S(2)}, u32[]{:S(2)}) collective-permute-start(f32[16,32,128]{2,1,0:T(8,128)S(1)} %get-tuple-element.32), channel_id=1, source_target_pairs={{0,8},{8,0},{16,24},{24,16},{1,9},{9,1},{17,25},{25,17},{2,10},{10... | collective-permute-start | bytes 786440 | tf_op jit(solution)/shard_map/ppermute | solution.py:257
  1436.8 52.7 %all-to-all-start.3 = ((bf16[8,1,16,8192]{3,2,1,0:T(8,128)(2,1)}), bf16[8,1,16,8192]{3,2,1,0:T(8,128)(2,1)S(1)}, u32[]{:S(2)}, u32[]{:S(2)}) async-start(bf16[8,1,16,8192]{3,2,1,0:T(8,128)(2,1)} %shard_map.86), calls=%async_computation.3 | async-start | bytes 4194304 | tf_op jit(solution)/shard_map/all_to_all | solution.py:55
  1454.2 18.3 %collective-permute-start.5 = (f32[7,32,128]{2,1,0:T(8,128)S(1)}, f32[7,32,128]{2,1,0:T(8,128)S(1)}, u32[]{:S(2)}, u32[]{:S(2)}) collective-permute-start(f32[7,32,128]{2,1,0:T(8,128)S(1)} %get-tuple-element.39), channel_id=1, source_target_pairs={{0,24},{8,16},{16,8},{24,0},{1,25},{9,17},{17,9},{25,1},{2,26},{10... | collective-permute-start | bytes 344072 | tf_op jit(solution)/shard_map/ppermute | solution.py:257
  1454.7 18.1 %collective-permute-start.4 = (f32[7,32,128]{2,1,0:T(8,128)S(1)}, f32[7,32,128]{2,1,0:T(8,128)S(1)}, u32[]{:S(2)}, u32[]{:S(2)}) collective-permute-start(f32[7,32,128]{2,1,0:T(8,128)S(1)} %get-tuple-element.38), channel_id=1, source_target_pairs={{0,16},{8,24},{16,0},{24,8},{1,17},{9,25},{17,1},{25,9},{2,18},{10... | collective-permute-start | bytes 344072 | tf_op jit(solution)/shard_map/ppermute | solution.py:257
  1455.6 17.1 %collective-permute-start.3 = (f32[7,32,128]{2,1,0:T(8,128)S(1)}, f32[7,32,128]{2,1,0:T(8,128)S(1)}, u32[]{:S(2)}, u32[]{:S(2)}) collective-permute-start(f32[7,32,128]{2,1,0:T(8,128)S(1)} %get-tuple-element.37), channel_id=1, source_target_pairs={{0,8},{8,0},{16,24},{24,16},{1,9},{9,1},{17,25},{25,17},{2,10},{10... | collective-permute-start | bytes 344072 | tf_op jit(solution)/shard_map/ppermute | solution.py:257
  1470.8 22.4 %collective-permute-start.8 = (f32[8,32,128]{2,1,0:T(8,128)S(1)}, f32[8,32,128]{2,1,0:T(8,128)S(1)}, u32[]{:S(2)}, u32[]{:S(2)}) collective-permute-start(f32[8,32,128]{2,1,0:T(8,128)S(1)} %get-tuple-element.43), channel_id=1, source_target_pairs={{0,24},{8,16},{16,8},{24,0},{1,25},{9,17},{17,9},{25,1},{2,26},{10... | collective-permute-start | bytes 393224 | tf_op jit(solution)/shard_map/ppermute | solution.py:257
  1471.6 22.4 %collective-permute-start.7 = (f32[8,32,128]{2,1,0:T(8,128)S(1)}, f32[8,32,128]{2,1,0:T(8,128)S(1)}, u32[]{:S(2)}, u32[]{:S(2)}) collective-permute-start(f32[8,32,128]{2,1,0:T(8,128)S(1)} %get-tuple-element.42), channel_id=1, source_target_pairs={{0,16},{8,24},{16,0},{24,8},{1,17},{9,25},{17,1},{25,9},{2,18},{10... | collective-permute-start | bytes 393224 | tf_op jit(solution)/shard_map/ppermute | solution.py:257
  1472.5 21.4 %collective-permute-start.6 = (f32[8,32,128]{2,1,0:T(8,128)S(1)}, f32[8,32,128]{2,1,0:T(8,128)S(1)}, u32[]{:S(2)}, u32[]{:S(2)}) collective-permute-start(f32[8,32,128]{2,1,0:T(8,128)S(1)} %get-tuple-element.41), channel_id=1, source_target_pairs={{0,8},{8,0},{16,24},{24,16},{1,9},{9,1},{17,25},{25,17},{2,10},{10... | collective-permute-start | bytes 393224 | tf_op jit(solution)/shard_map/ppermute | solution.py:257
  1492.0 3.2 collective-permute-start.11
  1492.1 3.8 collective-permute-start.10
  1493.3 2.7 collective-permute-start.9

commit v2 on v1

--- a/solution.py
+++ b/solution.py
@@ -117,7 +117,8 @@
     )(grid_map, factor)
 
 
-def send_kernel(activate, x_ref, w_ref, out_ref, wide_ref):
+def send_kernel(activate, x_ref, w_ref, *refs):
+    out_refs, wide_ref = refs[:-1], refs[-1]
     blocks, size = w_ref.shape[0], w_ref.shape[-1]
     dests, count = w_ref.shape[1], w_ref.shape[2]
     width = dests * count
@@ -134,15 +135,23 @@
         for n in range(count):
             for k in range(pieces):
                 rows = wide_ref[k, pl.ds(dest * count + n, blocks, stride=pitch), :]
-                out_ref[dest, n, :, k * lane_count : (k + 1) * lane_count] = rows.astype(bf16)
-
-
-def send_part(x, factor, rows, part, activate, tile):
+                out = out_refs[0].at[dest] if len(out_refs) == 1 else out_refs[dest]
+                out[n, :, k * lane_count : (k + 1) * lane_count] = rows.astype(bf16)
+
+
+def send_part(x, factor, rows, part, activate, tile, apart=False):
     blocks, wide, _, size = factor.shape
     (start, stop), (first, last) = rows, part
     count, length = last - first, stop - start
     width = wide * count
     taken = factor[:, :, first:last]
+    if apart:
+        taken = jnp.take(taken, lax.axis_index("wide") ^ jnp.arange(wide, dtype=jnp.int32), axis=1)
+        out_specs = [pl.BlockSpec((count, blocks, tile), lambda i: (0, 0, i))] * wide
+        out_shape = [jax.ShapeDtypeStruct((count, blocks, length), bf16)] * wide
+    else:
+        out_specs = pl.BlockSpec((wide, count, blocks, tile), lambda i: (0, 0, 0, i))
+        out_shape = jax.ShapeDtypeStruct((wide, count, blocks, length), bf16)
     pitch = -(-width // 8) * 8 + 8
     return pl.pallas_call(
         functools.partial(send_kernel, activate),
@@ -151,8 +160,8 @@
             pl.BlockSpec((tile, blocks * size), lambda i: (start // tile + i, 0)),
             pl.BlockSpec((blocks, wide, count, size), lambda i: (0, 0, 0, 0)),
         ],
-        out_specs=pl.BlockSpec((wide, count, blocks, tile), lambda i: (0, 0, 0, i)),
-        out_shape=jax.ShapeDtypeStruct((wide, count, blocks, length), bf16),
+        out_specs=out_specs,
+        out_shape=out_shape,
         scratch_shapes=[pltpu.VMEM((tile // lane_count, blocks * pitch, lane_count), f32)],
         cost_estimate=cost(
             2 * length * blocks * width * size,
@@ -163,38 +172,60 @@
     )(x, taken)
 
 
-def right_kernel(map_ref, received_ref, g_ref, *refs):
-    out_refs, rows_ref = refs[:-1], refs[-1]
-    size = g_ref.shape[1]
-    total = dot(received_ref[:, 0].reshape(size, received_ref.shape[3]), g_ref[...], 1, 0)
-    order = map_ref[0:1, :] // size
-    pick = jnp.where(lax.broadcasted_iota(jnp.int32, (size, size), 0) == order, 1.0, 0.0)
+def right_kernel(apart, map_ref, *refs):
+    count = apart or 1
+    received_refs, g_ref, out_refs, rows_ref = refs[:count], refs[count], refs[count + 1 : -1], refs[-1]
+    size, length = g_ref.shape[1], g_ref.shape[0]
+    block = lax.broadcasted_iota(jnp.int32, (size, size), 0)
+    if apart:
+        rows = jnp.concatenate([ref[0] for ref in received_refs], axis=0)
+        block = block ^ (lax.axis_index("wide") * received_refs[0].shape[1])
+    else:
+        rows = received_refs[0][:, 0].reshape(size, length)
+    total = dot(rows, g_ref[...], 1, 0)
+    pick = jnp.where(block == map_ref[0:1, :] // size, 1.0, 0.0)
     rows_ref[...] = dot(pick, total, 0, 0, lax.Precision.HIGHEST)
     share_out(rows_ref, out_refs, 0)
 
 
 def right_part(grid_map, received, cotangent, part, first):
     dp = lax.axis_size("dp")
-    wide, _, blocks, length = received.shape
     size = grid_map.shape[0]
+    length = cotangent.shape[0]
     count, skip = part[1] - part[0], part[0] - first
+    if isinstance(received, list):
+        apart = len(received)
+        blocks = received[0].shape[1]
+        specs = [pl.BlockSpec((1, blocks, length), lambda n: (skip + n, 0, 0))] * apart
+    else:
+        apart = 0
+        wide, _, blocks, _ = received.shape
+        specs = [pl.BlockSpec((wide, 1, blocks, length), lambda n: (0, skip + n, 0, 0))]
+        received = [received]
+    out_specs = [pl.BlockSpec((1, size // dp, size), lambda n: (n, 0, 0))] * dp
+    out_shape = [jax.ShapeDtypeStruct((count, size // dp, size), f32)] * dp
     return pl.pallas_call(
-        right_kernel,
+        functools.partial(right_kernel, apart),
         grid=(count,),
         in_specs=[
             pl.BlockSpec((size, size), lambda n: (0, 0)),
-            pl.BlockSpec((wide, 1, blocks, length), lambda n: (0, skip + n, 0, 0)),
+            *specs,
             pl.BlockSpec((length, size), lambda n: (0, part[0] + n)),
         ],
-        out_specs=[pl.BlockSpec((1, size // dp, size), lambda n: (n, 0, 0))] * dp,
-        out_shape=[jax.ShapeDtypeStruct((count, size // dp, size), f32)] * dp,
+        out_specs=out_specs,
+        out_shape=out_shape,
         scratch_shapes=[pltpu.VMEM((size, size), f32)],
         cost_estimate=cost(2 * count * size * size * length, 4 * count * size * length),
         compiler_params=params(1),
-    )(grid_map, received, cotangent)
-
-
-def back_kernel(has_total, received_ref, x_ref, w_ref, *refs):
+    )(grid_map, *received, cotangent)
+
+
+def back_kernel(apart, has_total, *refs):
+    count = apart or 1
+    received_refs, x_ref, w_ref = refs[:count], refs[count], refs[count + 1]
+    refs = refs[count + 2 :]
+    if apart:
+        *refs, turned_ref = refs
     if has_total:
         _, earlier_ref, rows_ref, total_ref = refs
     else:
@@ -212,30 +243,44 @@
     for b in range(blocks):
         x = x_ref[:, b * size : (b + 1) * size]
         slope = gelu_slope(dot(w_ref[b], x, 1, 1))
-        d_hidden = received_ref[:, b].reshape(size, tile).astype(f32)
+        if apart:
+            for s, ref in enumerate(received_refs):
+                first = (lax.axis_index("wide") ^ s) * blocks
+                turned_ref[pl.ds(pl.multiple_of(first, blocks), blocks), :] = ref[b]
+            d_hidden = turned_ref[...].astype(f32)
+        else:
+            d_hidden = received_refs[0][:, b].reshape(size, tile).astype(f32)
         d_pre = (d_hidden * slope).astype(bf16)
         total_ref[b] += dot(d_pre, x, 1, 0)
         rows_ref[:, b * size : (b + 1) * size] = dot(d_pre, w_ref[b], 0, 0).astype(bf16)
 
 
 def back_part(received, tokens, factor, rows, earlier, tile):
-    wide, blocks, _, length = received.shape
-    size = factor.shape[1]
+    blocks, size, _ = factor.shape
+    length = rows[1] - rows[0]
     start = rows[0] // tile
     whole_factor = pl.BlockSpec((blocks, size, size), lambda i: (0, 0, 0))
-    in_specs = [
-        pl.BlockSpec((wide, blocks, blocks, tile), lambda i: (0, 0, 0, i)),
+    scratch = []
+    if isinstance(received, list):
+        apart = len(received)
+        specs = [pl.BlockSpec((blocks, blocks, tile), lambda i: (0, 0, i))] * apart
+        scratch = [pltpu.VMEM((size, tile), bf16)]
+    else:
+        apart = 0
+        specs = [pl.BlockSpec((received.shape[0], blocks, blocks, tile), lambda i: (0, 0, 0, i))]
+        received = [received]
+    in_specs = specs + [
         pl.BlockSpec((tile, blocks * size), lambda i: (start + i, 0)),
         whole_factor,
     ]
-    operands = [received, tokens, factor]
+    operands = [*received, tokens, factor]
     aliases = {}
     if earlier is not None:
         in_specs += [pl.BlockSpec(memory_space=pl.ANY), whole_factor]
         operands += list(earlier)
-        aliases = {3: 0}
+        aliases = {len(received) + 2: 0}
     return pl.pallas_call(
-        functools.partial(back_kernel, earlier is not None),
+        functools.partial(back_kernel, apart, earlier is not None),
         grid=(length // tile,),
         in_specs=in_specs,
         out_specs=[pl.BlockSpec((tile, blocks * size), lambda i: (start + i, 0)), whole_factor],
@@ -243,9 +288,10 @@
             jax.ShapeDtypeStruct(tokens.shape, bf16),
             jax.ShapeDtypeStruct((blocks, size, size), f32),
         ],
+        scratch_shapes=scratch,
         input_output_aliases=aliases,
         cost_estimate=cost(
-            6 * length * blocks * size * size, 6 * length * blocks * size, length * blocks * size
+            back_hint * 6 * length * blocks * size * size, 6 * length * blocks * size, length * blocks * size
         ),
         compiler_params=params(1),
     )(*operands)
@@ -265,50 +311,57 @@
     wide = lax.axis_size("wide")
     tile = 512
 
+    by_dest = (blocks, wide, blocks, size)
+    everything = (0, row_count)
+    far, near = range(wide // 2, wide), range(1, wide // 2)
+    head, body = cuts(row_count, row_weights, tile)
+    main, filler, final = cuts(blocks, block_weights)
+
+    def move(piece, s):
+        return lax.ppermute(piece, "wide", [(i, i ^ s) for i in range(wide)])
+
     grid_map = column_map.reshape(size, size)
     right_full = lax.all_gather(right_factor, "dp", axis=1, tiled=True)
-    right_sent = ordered(right_sent_kernel, grid_map, right_full)
+    right_sent = ordered(right_sent_kernel, grid_map, right_full).reshape(by_dest)
+    send = send_part(cotangent, right_sent, head, (0, blocks), False, tile)
+    got_head = exchange(send)
+    right_sent = after(right_sent, send)
+    got_body = exchange(after(send_part(cotangent, right_sent, body, (0, blocks), False, tile), got_head))
+
     left_full = lax.all_gather(left_factor, "dp", axis=1, tiled=True)
     left_sent = ordered(left_sent_kernel, grid_map, left_full)
-    by_dest = (blocks, wide, blocks, size)
-    everything = (0, row_count)
-
-    row_cuts = cuts(row_count, row_weights, tile)
-    block_cuts = cuts(blocks, block_weights)
-    last, arrived = None, []
-    for rows in row_cuts:
-        send = send_part(cotangent, right_sent.reshape(by_dest), rows, (0, blocks), False, tile)
-        last = exchange(after(send, last))
-        arrived.append(last)
-
-    received = []
-    for part in block_cuts[:-1]:
-        send = send_part(tokens, left_sent.reshape(by_dest), everything, part, True, tile)
-        last = exchange(after(send, last))
-        received.append(last)
-
-    earlier = None
-    for rows, got in zip(row_cuts, arrived):
-        earlier = back_part(got, tokens, left_sent, rows, earlier, tile)
-    grad_tokens, left_total = earlier
-    left_share = sum_over_dp(left_done(grid_map, left_total))
-
-    part = block_cuts[-1]
-    send = send_part(tokens, left_sent.reshape(by_dest), everything, part, True, tile)
-    last = exchange(after(send, (last, left_share)))
-
-    shares = []
-    for (first, stop), got in zip(block_cuts, received):
-        half = (first + stop) // 2
-        for piece in ((first, half), (half, stop)):
-            if piece[1] > piece[0]:
-                shares.append(sum_over_dp(right_part(grid_map, got, cotangent, piece, first)))
-    shares.append(sum_over_dp(right_part(grid_map, last, cotangent, part, part[0])))
+    left_by_dest = left_sent.reshape(by_dest)
+    apart = send_part(tokens, left_by_dest, everything, filler, True, tile, True)
+    got_filler = {0: apart[0], **{s: move(apart[s], s) for s in far}}
+    rest = send_part(tokens, after(left_by_dest, apart[0]), everything, main, True, tile)
+    got_main = exchange(after(rest, got_body))
+
+    arrived = tuple(got_filler[s] for s in far)
+    left_then = after(left_sent, arrived)
+    earlier = back_part(got_head, tokens, left_then, head, None, tile)
+    got_filler |= {s: move(after(apart[s], earlier[1]), s) for s in near}
+    grad_tokens, left_total = back_part(got_body, tokens, left_sent, body, earlier, tile)
+    arrived = tuple(got_filler[s] for s in near)
+    left_share = sum_over_dp(left_done(after(grid_map, arrived), left_total))
+    send = send_part(tokens, left_by_dest, everything, final, True, tile)
+    got_final = exchange(after(send, (got_main, left_share)))
+
+    def share(part, got, begin):
+        return sum_over_dp(right_part(grid_map, got, cotangent, part, begin))
+
+    middle = (main[0] + main[1]) // 2
+    shares = [
+        share((main[0], middle), got_main, main[0]),
+        share((middle, main[1]), got_main, main[0]),
+        share(filler, [got_filler[s] for s in range(wide)], filler[0]),
+        share(final, got_final, final[0]),
+    ]
     return (grad_tokens, left_share, jnp.concatenate(shares, axis=0))
 
 
+back_hint = 41.75
 row_weights = (1, 15)
-block_weights = (15, 1)
+block_weights = (14, 1, 1)
 
 
 def plain(tokens, cotangent, left_factor, right_factor, column_map):
@@ -357,8 +410,10 @@
 def shards(*args):
     blocks, size = args[2].shape[0], args[2].shape[2]
     dp = lax.axis_size("dp")
-    fits = blocks % 16 == 0 and size == lane_count and dp & (dp - 1) == 0 and size % (8 * dp) == 0
-    return (with_kernels if fits else plain)(*args)
+    wide = lax.axis_size("wide")
+    powers = dp & (dp - 1) == 0 and wide & (wide - 1) == 0 and wide > 1
+    fits = blocks % 16 == 0 and blocks & (blocks - 1) == 0 and size == lane_count and size % (8 * dp) == 0
+    return (with_kernels if fits and powers else plain)(*args)
 
 
 def solution(mesh):

time: 1500 us -> 1490 us (level)
  waiting for transfers between devices: 1180 us -> 1080 us
  starting transfers between devices: 31.8 us -> 131 us
  Pallas kernels: 267 us -> 249 us
    all_to_all x4, waiting for transfers between devices: 1180 us -> 697 us  [exchange(): return lax.all_to_all(send, 'wide', split_axis=0, concat_axis=0, tiled=True)]
    ppermute x0 -> x7, waiting for transfers between devices: none -> 384 us  [move(): return lax.ppermute(piece, 'wide', [(i, i ^ s) for i in range(wide)])]
    ppermute x0 -> x7, starting transfers between devices: none -> 97.6 us  [move(): return lax.ppermute(piece, 'wide', [(i, i ^ s) for i in range(wide)])]
    pallas_call x4 -> x5, Pallas kernels: 139 us -> 119 us  [send_part(): pl.pallas_call(functools.partial(send_kernel, activate), grid=(length //...]
    pallas_call x5 -> x6, Pallas kernels: 126 us -> 128 us  [the longest x2 96.1 us: back_part(): pl.pallas_call(functools.partial(back_kernel, apart, earlier is not None)...]
  transfers between devices with their start and end apart: 16 -> 26, of which waited for: 6 -> 12; matrix products, arithmetic and copies ran while one was open for 0% -> 0% of each run, Pallas kernels for 18% -> 16%
where the time goes in v2:
time: 1490 us
  waiting for transfers between devices  1080 us (72%)
  Pallas kernels  249 us (17%)
  starting transfers between devices  131 us (9%)
  blocking collectives  15.6 us (1%)
    all_to_all x4, waiting for transfers between devices, exchange(): return lax.all_to_all(send, 'wide', split_axis=0, concat_axis=0, tiled=True)  697 us
    ppermute x7, waiting for transfers between devices, move(): return lax.ppermute(piece, 'wide', [(i, i ^ s) for i in range(wide)])  384 us
    pallas_call x5, Pallas kernels, send_part(): pl.pallas_call(functools.partial(send_kernel, activate), grid=(length //...  119 us
    ppermute x7, starting transfers between devices, move(): return lax.ppermute(piece, 'wide', [(i, i ^ s) for i in range(wide)])  97.6 us
    pallas_call x2, Pallas kernels, back_part(): pl.pallas_call(functools.partial(back_kernel, apart, earlier is not None)...  96.1 us
    pallas_call x4, Pallas kernels, right_part(): pl.pallas_call(functools.partial(right_kernel, apart), grid=(count,), in_...  31.6 us
  transfers between devices with their start and end apart: 26, of which 12 were waited for; matrix products, arithmetic and copies ran while one was open for 0% of the time, Pallas kernels for 16%

profile of v2, /device:TPU:0, one launch (start us, length us, event | category | flops | bytes accessed | tf_op | source)
XLA Modules:
  0.0 1487.3 jit_solution(873707352397178616)
XLA Ops:
  0.6 8.8 all_gather.6.factor_ref
  9.5 0.8 copy-done
  10.6 4.5 shard_map.77
  15.1 5.8 all-to-all-start
  20.9 32.4 %shard_map.78 = bf16[8,16,16,7680]{3,2,1,0:T(8,128)(2,1)} custom-call(bf16[8192,2048]{1,0:T(8,128)(2,1)} %refs_1_.9, bf16[16,8,16,128]{3,2,1,0:T(8,128)(2,1)S(1)} %bitcast.13), custom_call_target="tpu_custom_call" | custom-call | flops 4026531840 | bytes 62914560 | tf_op jit(solution)/shard_map/pallas_call | solution.py:156
  53.4 16.3 %all-to-all-done.refs_0_ = bf16[8,16,16,512]{3,2,1,0:T(8,128)(2,1)S(1)} async-done(((bf16[8,16,16,512]{3,2,1,0:T(8,128)(2,1)}), bf16[8,16,16,512]{3,2,1,0:T(8,128)(2,1)S(1)}, u32[]{:S(2)}, u32[]{:S(2)}) %all-to-all-start) | async-done | bytes 2097184 | tf_op jit(solution)/shard_map/all_to_all | solution.py:55
  69.7 6.9 all-to-all-start.1
  76.6 6.8 all_gather.7.factor_ref
  84.8 21.4 %shard_map.80 = (bf16[1,16,8192]{2,1,0:T(8,128)(2,1)S(1)}, bf16[1,16,8192]{2,1,0:T(8,128)(2,1)S(1)}, bf16[1,16,8192]{2,1,0:T(8,128)(2,1)S(1)}, bf16[1,16,8192]{2...) custom-call(bf16[8192,2048]{1,0:T(8,128)(2,1)} %x_ref.9, ...), custom_call_target="tpu_custom_call" | custom-call | flops 268435456 | bytes 35651584 | tf_op jit(solution)/shard_map/pallas_call | solution.py:156
  106.9 0.7 copy-done.11
  107.6 0.7 copy-done.13
  108.3 2.8 collective-permute-start
  111.1 1.4 collective-permute-start.1
  112.5 3.3 collective-permute-start.2
  116.0 39.6 %shard_map.84 = bf16[8,14,16,8192]{3,2,1,0:T(8,128)(2,1)} custom-call(bf16[8192,2048]{1,0:T(8,128)(2,1)} %x_ref.9, bf16[16,8,14,128]{3,2,1,0:T(8,128)(2,1)S(1)} %bitcast.15), custom_call_target="tpu_custom_call" | custom-call | flops 3758096384 | bytes 62914560 | tf_op jit(solution)/shard_map/pallas_call | solution.py:156
  155.6 622.4 %all-to-all-done.1.refs_0_ = bf16[8,16,16,7680]{3,2,1,0:T(8,128)(2,1)} async-done(((bf16[8,16,16,7680]{3,2,1,0:T(8,128)(2,1)}), bf16[8,16,16,7680]{3,2,1,0:T(8,128)(2,1)}, u32[]{:S(2)}, u32[]{:S(2)}) %all-to-all-start.1) | async-done | bytes 31457312 | tf_op jit(solution)/shard_map/all_to_all | solution.py:55
  777.9 6.9 all-to-all-start.2
  784.9 81.3 %collective-permute-done.1.refs_5_ = bf16[1,16,8192]{2,1,0:T(8,128)(2,1)S(1)} collective-permute-done((bf16[1,16,8192]{2,1,0:T(8,128)(2,1)}, bf16[1,16,8192]{2,1,0:T(8,128)(2,1)S(1)}, u32[]{:S(2)}, u32[]{:S(2)}) %collective-permute-start.1) | collective-permute-done | bytes 262176 | tf_op jit(solution)/shard_map/ppermute | solution.py:321
  866.2 8.4 shard_map.81
  874.6 90.0 %collective-permute-start.5 = (bf16[1,16,8192]{2,1,0:T(8,128)(2,1)S(1)}, bf16[1,16,8192]{2,1,0:T(8,128)(2,1)S(1)}, u32[]{:S(2)}, u32[]{:S(2)}) collective-permute-start(bf16[1,16,8192]{2,1,0:T(8,128)(2,1)S(1)} %copy-done.12), channel_id=1, source_target_pairs={{0,2},{1,3},{2,0},{3,1},{4,6},{5,7},{6,4},{7,5},{8,10},{9,11},{10,... | collective-permute-start | bytes 786440 | tf_op jit(solution)/shard_map/ppermute | solution.py:321
  964.6 63.0 %collective-permute-done.4.refs_1_ = bf16[1,16,8192]{2,1,0:T(8,128)(2,1)S(1)} collective-permute-done((bf16[1,16,8192]{2,1,0:T(8,128)(2,1)S(1)}, bf16[1,16,8192]{2,1,0:T(8,128)(2,1)S(1)}, u32[]{:S(2)}, u32[]{:S(2)}) %collective-permute-start.4) | collective-permute-done | bytes 262176 | tf_op jit(solution)/shard_map/ppermute | solution.py:321
  1027.6 236.7 %collective-permute-done.5.refs_2_ = bf16[1,16,8192]{2,1,0:T(8,128)(2,1)S(1)} collective-permute-done((bf16[1,16,8192]{2,1,0:T(8,128)(2,1)S(1)}, bf16[1,16,8192]{2,1,0:T(8,128)(2,1)S(1)}, u32[]{:S(2)}, u32[]{:S(2)}) %collective-permute-start.5) | collective-permute-done | bytes 262176 | tf_op jit(solution)/shard_map/ppermute | solution.py:321
  1264.4 2.8 collective-permute-done.6.refs_3_
  1267.2 87.7 %shard_map.82 = (bf16[8192,2048]{1,0:T(8,128)(2,1)}, f32[16,128,128]{2,1,0:T(8,128)S(1)}) custom-call(bf16[8,16,16,7680]{3,2,1,0:T(8,128)(2,1)} %all-to-all-done.1.refs_0_, bf16[8192,2048]{1,0:T(8,128)(2,1)} %x_ref.9, bf16[16,128,128]{2,1,0:T(8,128)(2,1)S(1)} %shard_map.79.refs_2_, ...), custom_call_target="tpu_custom_call", output_to_operand_aliasing={{0}: (3, {})} | custom-call | flops 504323112960 | bytes 94371840 | tf_op jit(solution)/shard_map/pallas_call | solution.py:282
  1354.9 1.2 shard_map.83
  1356.2 1.2 collective-permute-start.8
  1357.3 0.7 collective-permute-start.7
  1358.0 21.3 %shard_map.88 = bf16[8,1,16,8192]{3,2,1,0:T(8,128)(2,1)} custom-call(bf16[8192,2048]{1,0:T(8,128)(2,1)} %x_ref.9, bf16[16,8,1,128]{3,2,1,0:T(2,128)(2,1)S(1)} %get-tuple-element.87.w_ref), custom_call_target="tpu_custom_call" | custom-call | flops 268435456 | bytes 35651584 | tf_op jit(solution)/shard_map/pallas_call | solution.py:156
  1379.4 0.8 add_add_fusion
  1380.1 48.4 %all-to-all-done.2.refs_0_ = bf16[8,14,16,8192]{3,2,1,0:T(8,128)(2,1)} async-done(((bf16[8,14,16,8192]{3,2,1,0:T(8,128)(2,1)}), bf16[8,14,16,8192]{3,2,1,0:T(8,128)(2,1)}, u32[]{:S(2)}, u32[]{:S(2)}) %all-to-all-start.2) | async-done | bytes 29360160 | tf_op jit(solution)/shard_map/all_to_all | solution.py:55
  1428.5 3.8 all-to-all-start.3
  1432.4 0.9 copy-done.8
  1433.3 2.7 shard_map.87
  1436.2 1.1 collective-permute-start.17
  1437.3 0.7 collective-permute-start.16
  1438.0 1.3 collective-permute-done.18
  1440.0 13.2 shard_map.86
  1453.2 1.0 collective-permute-start.15
  1454.2 0.9 collective-permute-start.14
  1455.1 13.1 shard_map.85
  1468.3 1.3 collective-permute-start.12
  1469.6 0.9 collective-permute-start.11
  1470.5 9.5 all-to-all-done.3.refs_0_
  1480.1 2.5 shard_map.89
  1482.7 1.1 collective-permute-start.20
  1483.9 0.7 collective-permute-start.19
  1484.6 1.3 collective-permute-done.21
  1486.5 0.7 pad_maximum_fusion
  (65 shorter events, 4.2 us)
Async XLA Ops:
  9.5 0.8 copy-start
  15.1 54.6 %all-to-all-start = ((bf16[8,16,16,512]{3,2,1,0:T(8,128)(2,1)}), bf16[8,16,16,512]{3,2,1,0:T(8,128)(2,1)S(1)}, u32[]{:S(2)}, u32[]{:S(2)}) async-start(bf16[8,16,16,512]{3,2,1,0:T(8,128)(2,1)} %shard_map.77), calls=%async_computation | async-start | bytes 4194304 | tf_op jit(solution)/shard_map/all_to_all | solution.py:55
  53.4 23.3 %copy-start.15 = (bf16[16,32,128]{2,1,0:T(8,128)(2,1)S(1)}, bf16[16,32,128]{2,1,0:T(8,128)(2,1)}, u32[]{:S(2)}) copy-start(bf16[16,32,128]{2,1,0:T(8,128)(2,1)} %param.7) | copy-start | bytes 393220
  53.4 30.0 %copy-start.1 = (s32[16384]{0:T(1024)S(1)}, s32[16384]{0:T(1024)}, u32[]{:S(2)}) copy-start(s32[16384]{0:T(1024)} %param.9) | copy-start | bytes 196612
  69.7 708.3 %all-to-all-start.1 = ((bf16[8,16,16,7680]{3,2,1,0:T(8,128)(2,1)}), bf16[8,16,16,7680]{3,2,1,0:T(8,128)(2,1)}, u32[]{:S(2)}, u32[]{:S(2)}) async-start(bf16[8,16,16,7680]{3,2,1,0:T(8,128)(2,1)} %shard_map.78), calls=%async_computation.1 | async-start | bytes 62914560 | tf_op jit(solution)/shard_map/all_to_all | solution.py:55
  106.2 0.7 copy-start.9
  106.9 0.7 copy-start.11
  107.6 0.7 copy-start.13
  108.3 676.6 %collective-permute-start = (bf16[1,16,8192]{2,1,0:T(8,128)(2,1)}, bf16[1,16,8192]{2,1,0:T(8,128)(2,1)S(1)}, u32[]{:S(2)}, u32[]{:S(2)}) collective-permute-start(bf16[1,16,8192]{2,1,0:T(8,128)(2,1)} %get-tuple-element.47), channel_id=1, source_target_pairs={{0,4},{1,5},{2,6},{3,7},{4,0},{5,1},{6,2},{7,3},{8,12},{9,13},{10,... | collective-permute-start | bytes 786440 | tf_op jit(solution)/shard_map/ppermute | solution.py:321
  111.1 755.1 %collective-permute-start.1 = (bf16[1,16,8192]{2,1,0:T(8,128)(2,1)}, bf16[1,16,8192]{2,1,0:T(8,128)(2,1)S(1)}, u32[]{:S(2)}, u32[]{:S(2)}) collective-permute-start(bf16[1,16,8192]{2,1,0:T(8,128)(2,1)} %get-tuple-element.48), channel_id=1, source_target_pairs={{0,5},{1,4},{2,7},{3,6},{4,1},{5,0},{6,3},{7,2},{8,13},{9,12},{10,... | collective-permute-start | bytes 786440 | tf_op jit(solution)/shard_map/ppermute | solution.py:321
  112.5 753.6 %collective-permute-start.2 = (bf16[1,16,8192]{2,1,0:T(8,128)(2,1)}, bf16[1,16,8192]{2,1,0:T(8,128)(2,1)}, u32[]{:S(2)}, u32[]{:S(2)}) collective-permute-start(bf16[1,16,8192]{2,1,0:T(8,128)(2,1)} %get-tuple-element.49), channel_id=1, source_target_pairs={{0,6},{1,7},{2,4},{3,5},{4,2},{5,3},{6,0},{7,1},{8,14},{9,15},{10,... | collective-permute-start | bytes 786440 | tf_op jit(solution)/shard_map/ppermute | solution.py:321
  115.8 750.3 %collective-permute-start.3 = (bf16[1,16,8192]{2,1,0:T(8,128)(2,1)}, bf16[1,16,8192]{2,1,0:T(8,128)(2,1)}, u32[]{:S(2)}, u32[]{:S(2)}) collective-permute-start(bf16[1,16,8192]{2,1,0:T(8,128)(2,1)} %get-tuple-element.50), channel_id=1, source_target_pairs={{0,7},{1,6},{2,5},{3,4},{4,3},{5,2},{6,1},{7,0},{8,15},{9,14},{10,... | collective-permute-start | bytes 786440 | tf_op jit(solution)/shard_map/ppermute | solution.py:321
  777.9 650.6 %all-to-all-start.2 = ((bf16[8,14,16,8192]{3,2,1,0:T(8,128)(2,1)}), bf16[8,14,16,8192]{3,2,1,0:T(8,128)(2,1)}, u32[]{:S(2)}, u32[]{:S(2)}) async-start(bf16[8,14,16,8192]{3,2,1,0:T(8,128)(2,1)} %shard_map.84), calls=%async_computation.2 | async-start | bytes 58720256 | tf_op jit(solution)/shard_map/all_to_all | solution.py:55
  784.8 89.8 %copy-start.14 = (bf16[1,16,8192]{2,1,0:T(8,128)(2,1)S(1)}, bf16[1,16,8192]{2,1,0:T(8,128)(2,1)}, u32[]{:S(2)}) copy-start(bf16[1,16,8192]{2,1,0:T(8,128)(2,1)} %copy-done.13) | copy-start | bytes 786436
  784.9 89.8 %copy-start.12 = (bf16[1,16,8192]{2,1,0:T(8,128)(2,1)S(1)}, bf16[1,16,8192]{2,1,0:T(8,128)(2,1)}, u32[]{:S(2)}) copy-start(bf16[1,16,8192]{2,1,0:T(8,128)(2,1)} %copy-done.11) | copy-start | bytes 786436
  784.9 179.7 %copy-start.10 = (bf16[1,16,8192]{2,1,0:T(8,128)(2,1)S(1)}, bf16[1,16,8192]{2,1,0:T(8,128)(2,1)}, u32[]{:S(2)}) copy-start(bf16[1,16,8192]{2,1,0:T(8,128)(2,1)} %copy-done.9) | copy-start | bytes 786436
  874.6 153.0 %collective-permute-start.4 = (bf16[1,16,8192]{2,1,0:T(8,128)(2,1)S(1)}, bf16[1,16,8192]{2,1,0:T(8,128)(2,1)S(1)}, u32[]{:S(2)}, u32[]{:S(2)}) collective-permute-start(bf16[1,16,8192]{2,1,0:T(8,128)(2,1)S(1)} %copy-done.14), channel_id=1, source_target_pairs={{0,1},{1,0},{2,3},{3,2},{4,5},{5,4},{6,7},{7,6},{8,9},{9,8},{10,11... | collective-permute-start | bytes 786440 | tf_op jit(solution)/shard_map/ppermute | solution.py:321
  874.6 389.8 %collective-permute-start.5 = (bf16[1,16,8192]{2,1,0:T(8,128)(2,1)S(1)}, bf16[1,16,8192]{2,1,0:T(8,128)(2,1)S(1)}, u32[]{:S(2)}, u32[]{:S(2)}) collective-permute-start(bf16[1,16,8192]{2,1,0:T(8,128)(2,1)S(1)} %copy-done.12), channel_id=1, source_target_pairs={{0,2},{1,3},{2,0},{3,1},{4,6},{5,7},{6,4},{7,5},{8,10},{9,11},{10,... | collective-permute-start | bytes 786440 | tf_op jit(solution)/shard_map/ppermute | solution.py:321
  964.6 302.6 %collective-permute-start.6 = (bf16[1,16,8192]{2,1,0:T(8,128)(2,1)S(1)}, bf16[1,16,8192]{2,1,0:T(8,128)(2,1)S(1)}, u32[]{:S(2)}, u32[]{:S(2)}) collective-permute-start(bf16[1,16,8192]{2,1,0:T(8,128)(2,1)S(1)} %copy-done.10), channel_id=1, source_target_pairs={{0,3},{1,2},{2,1},{3,0},{4,7},{5,6},{6,5},{7,4},{8,11},{9,10},{10,... | collective-permute-start | bytes 786440 | tf_op jit(solution)/shard_map/ppermute | solution.py:321
  1027.6 327.3 %copy-start.3 = (bf16[1,16,8192]{2,1,0:T(8,128)(2,1)}, bf16[1,16,8192]{2,1,0:T(8,128)(2,1)S(1)}, u32[]{:S(2)}) copy-start(bf16[1,16,8192]{2,1,0:T(8,128)(2,1)S(1)} %collective-permute-done.4.refs_1_) | copy-start | bytes 786436
  1264.4 90.5 %copy-start.5 = (bf16[1,16,8192]{2,1,0:T(8,128)(2,1)}, bf16[1,16,8192]{2,1,0:T(8,128)(2,1)S(1)}, u32[]{:S(2)}) copy-start(bf16[1,16,8192]{2,1,0:T(8,128)(2,1)S(1)} %collective-permute-done.5.refs_2_) | copy-start | bytes 786436
  1267.2 87.7 %copy-start.7 = (bf16[1,16,8192]{2,1,0:T(8,128)(2,1)}, bf16[1,16,8192]{2,1,0:T(8,128)(2,1)S(1)}, u32[]{:S(2)}) copy-start(bf16[1,16,8192]{2,1,0:T(8,128)(2,1)S(1)} %collective-permute-done.6.refs_3_) | copy-start | bytes 786436
  1354.9 77.5 %copy-start.2 = (s32[16384]{0:T(1024)S(1)}, s32[16384]{0:T(1024)}, u32[]{:S(2)}) copy-start(s32[16384]{0:T(1024)} %param.9) | copy-start | bytes 196612
  1354.9 77.5 %copy-start.4 = (bf16[1,16,8192]{2,1,0:T(8,128)(2,1)S(1)}, bf16[1,16,8192]{2,1,0:T(8,128)(2,1)}, u32[]{:S(2)}) copy-start(bf16[1,16,8192]{2,1,0:T(8,128)(2,1)} %copy-done.3) | copy-start | bytes 786436
  1354.9 77.5 %copy-start.6 = (bf16[1,16,8192]{2,1,0:T(8,128)(2,1)S(1)}, bf16[1,16,8192]{2,1,0:T(8,128)(2,1)}, u32[]{:S(2)}) copy-start(bf16[1,16,8192]{2,1,0:T(8,128)(2,1)} %copy-done.5) | copy-start | bytes 786436
  1356.1 23.3 %collective-permute-start.9 = (f32[16,32,128]{2,1,0:T(8,128)S(1)}, f32[16,32,128]{2,1,0:T(8,128)S(1)}, u32[]{:S(2)}, u32[]{:S(2)}) collective-permute-start(f32[16,32,128]{2,1,0:T(8,128)S(1)} %get-tuple-element.66), channel_id=1, source_target_pairs={{0,24},{8,16},{16,8},{24,0},{1,25},{9,17},{17,9},{25,1},{2,26},{10... | collective-permute-start | bytes 786440 | tf_op jit(solution)/shard_map/ppermute | solution.py:303
  1356.2 23.2 %collective-permute-start.8 = (f32[16,32,128]{2,1,0:T(8,128)S(1)}, f32[16,32,128]{2,1,0:T(8,128)S(1)}, u32[]{:S(2)}, u32[]{:S(2)}) collective-permute-start(f32[16,32,128]{2,1,0:T(8,128)S(1)} %get-tuple-element.65), channel_id=1, source_target_pairs={{0,16},{8,24},{16,0},{24,8},{1,17},{9,25},{17,1},{25,9},{2,18},{10... | collective-permute-start | bytes 786440 | tf_op jit(solution)/shard_map/ppermute | solution.py:303
  1357.3 22.0 %collective-permute-start.7 = (f32[16,32,128]{2,1,0:T(8,128)S(1)}, f32[16,32,128]{2,1,0:T(8,128)S(1)}, u32[]{:S(2)}, u32[]{:S(2)}) collective-permute-start(f32[16,32,128]{2,1,0:T(8,128)S(1)} %get-tuple-element.64), channel_id=1, source_target_pairs={{0,8},{8,0},{16,24},{24,16},{1,9},{9,1},{17,25},{25,17},{2,10},{10... | collective-permute-start | bytes 786440 | tf_op jit(solution)/shard_map/ppermute | solution.py:303
  1428.5 51.5 %all-to-all-start.3 = ((bf16[8,1,16,8192]{3,2,1,0:T(8,128)(2,1)}), bf16[8,1,16,8192]{3,2,1,0:T(8,128)(2,1)S(1)}, u32[]{:S(2)}, u32[]{:S(2)}) async-start(bf16[8,1,16,8192]{3,2,1,0:T(8,128)(2,1)} %shard_map.88), calls=%async_computation.3 | async-start | bytes 4194304 | tf_op jit(solution)/shard_map/all_to_all | solution.py:55
  1432.4 1.0 copy-start.8
  1436.1 3.2 collective-permute-start.18
  1436.2 3.8 collective-permute-start.17
  1437.3 2.7 collective-permute-start.16
  1453.2 17.3 %collective-permute-start.15 = (f32[7,32,128]{2,1,0:T(8,128)S(1)}, f32[7,32,128]{2,1,0:T(8,128)S(1)}, u32[]{:S(2)}, u32[]{:S(2)}) collective-permute-start(f32[7,32,128]{2,1,0:T(8,128)S(1)} %get-tuple-element.77), channel_id=1, source_target_pairs={{0,24},{8,16},{16,8},{24,0},{1,25},{9,17},{17,9},{25,1},{2,26},{10... | collective-permute-start | bytes 344072 | tf_op jit(solution)/shard_map/ppermute | solution.py:303
  1454.2 16.3 %collective-permute-start.14 = (f32[7,32,128]{2,1,0:T(8,128)S(1)}, f32[7,32,128]{2,1,0:T(8,128)S(1)}, u32[]{:S(2)}, u32[]{:S(2)}) collective-permute-start(f32[7,32,128]{2,1,0:T(8,128)S(1)} %get-tuple-element.76), channel_id=1, source_target_pairs={{0,16},{8,24},{16,0},{24,8},{1,17},{9,25},{17,1},{25,9},{2,18},{10... | collective-permute-start | bytes 344072 | tf_op jit(solution)/shard_map/ppermute | solution.py:303
  1455.1 15.4 %collective-permute-start.13 = (f32[7,32,128]{2,1,0:T(8,128)S(1)}, f32[7,32,128]{2,1,0:T(8,128)S(1)}, u32[]{:S(2)}, u32[]{:S(2)}) collective-permute-start(f32[7,32,128]{2,1,0:T(8,128)S(1)} %get-tuple-element.75), channel_id=1, source_target_pairs={{0,8},{8,0},{16,24},{24,16},{1,9},{9,1},{17,25},{25,17},{2,10},{10... | collective-permute-start | bytes 344072 | tf_op jit(solution)/shard_map/ppermute | solution.py:303
  1468.3 15.6 %collective-permute-start.12 = (f32[7,32,128]{2,1,0:T(8,128)S(1)}, f32[7,32,128]{2,1,0:T(8,128)S(1)}, u32[]{:S(2)}, u32[]{:S(2)}) collective-permute-start(f32[7,32,128]{2,1,0:T(8,128)S(1)} %get-tuple-element.73), channel_id=1, source_target_pairs={{0,24},{8,16},{16,8},{24,0},{1,25},{9,17},{17,9},{25,1},{2,26},{10... | collective-permute-start | bytes 344072 | tf_op jit(solution)/shard_map/ppermute | solution.py:303
  1469.6 15.0 %collective-permute-start.11 = (f32[7,32,128]{2,1,0:T(8,128)S(1)}, f32[7,32,128]{2,1,0:T(8,128)S(1)}, u32[]{:S(2)}, u32[]{:S(2)}) collective-permute-start(f32[7,32,128]{2,1,0:T(8,128)S(1)} %get-tuple-element.72), channel_id=1, source_target_pairs={{0,16},{8,24},{16,0},{24,8},{1,17},{9,25},{17,1},{25,9},{2,18},{10... | collective-permute-start | bytes 344072 | tf_op jit(solution)/shard_map/ppermute | solution.py:303
  1470.5 14.1 collective-permute-start.10
  1482.6 3.2 collective-permute-start.21
  1482.7 3.8 collective-permute-start.20
  1483.9 2.7 collective-permute-start.19

commit v3 on v2

--- a/solution.py
+++ b/solution.py
@@ -164,7 +164,7 @@
         out_shape=out_shape,
         scratch_shapes=[pltpu.VMEM((tile // lane_count, blocks * pitch, lane_count), f32)],
         cost_estimate=cost(
-            2 * length * blocks * width * size,
+            (send_hint if activate and count > 1 else 1) * 2 * length * blocks * width * size,
             2 * length * blocks * (size + width),
             length * blocks * width if activate else 0,
         ),
@@ -323,14 +323,17 @@
     grid_map = column_map.reshape(size, size)
     right_full = lax.all_gather(right_factor, "dp", axis=1, tiled=True)
     right_sent = ordered(right_sent_kernel, grid_map, right_full).reshape(by_dest)
-    send = send_part(cotangent, right_sent, head, (0, blocks), False, tile)
-    got_head = exchange(send)
-    right_sent = after(right_sent, send)
-    got_body = exchange(after(send_part(cotangent, right_sent, body, (0, blocks), False, tile), got_head))
-
-    left_full = lax.all_gather(left_factor, "dp", axis=1, tiled=True)
+    mixed = send_part(cotangent, right_sent, head, (0, blocks), False, tile, True)
+    got_head = {0: mixed[0], **{s: move(mixed[s], s) for s in far}}
+    right_sent = after(right_sent, mixed[0])
+    got_body = exchange(send_part(cotangent, right_sent, body, (0, blocks), False, tile))
+
+    arrived = tuple(got_head[s] for s in far)
+    left_full = lax.all_gather(after(left_factor, arrived), "dp", axis=1, tiled=True)
+    got_head |= {s: move(after(mixed[s], arrived), s) for s in near}
     left_sent = ordered(left_sent_kernel, grid_map, left_full)
     left_by_dest = left_sent.reshape(by_dest)
+    left_by_dest = after(left_by_dest, tuple(got_head[s] for s in near))
     apart = send_part(tokens, left_by_dest, everything, filler, True, tile, True)
     got_filler = {0: apart[0], **{s: move(apart[s], s) for s in far}}
     rest = send_part(tokens, after(left_by_dest, apart[0]), everything, main, True, tile)
@@ -338,7 +341,7 @@
 
     arrived = tuple(got_filler[s] for s in far)
     left_then = after(left_sent, arrived)
-    earlier = back_part(got_head, tokens, left_then, head, None, tile)
+    earlier = back_part([got_head[s] for s in range(wide)], tokens, left_then, head, None, tile)
     got_filler |= {s: move(after(apart[s], earlier[1]), s) for s in near}
     grad_tokens, left_total = back_part(got_body, tokens, left_sent, body, earlier, tile)
     arrived = tuple(got_filler[s] for s in near)
@@ -360,6 +363,7 @@
 
 
 back_hint = 41.75
+send_hint = 154.062
 row_weights = (1, 15)
 block_weights = (14, 1, 1)
 

time: 1490 us -> 1480 us (level)
  waiting for transfers between devices: 1080 us -> 889 us
  starting transfers between devices: 131 us -> 317 us
    all_to_all x4 -> x3, waiting for transfers between devices: 697 us -> 159 us  [exchange(): return lax.all_to_all(send, 'wide', split_axis=0, concat_axis=0, tiled=True)]
    ppermute x7 -> x14, waiting for transfers between devices: 384 us -> 725 us  [move(): return lax.ppermute(piece, 'wide', [(i, i ^ s) for i in range(wide)])]
    ppermute x7 -> x14, starting transfers between devices: 97.6 us -> 282 us  [move(): return lax.ppermute(piece, 'wide', [(i, i ^ s) for i in range(wide)])]
  transfers between devices with their start and end apart: 26 -> 32, of which waited for: 12 -> 14; matrix products, arithmetic and copies ran while one was open for 0% -> 0% of each run, Pallas kernels for 16% -> 17%
where the time goes in v3:
time: 1480 us
  waiting for transfers between devices  889 us (60%)
  starting transfers between devices  317 us (21%)
  Pallas kernels  248 us (17%)
  blocking collectives  15.6 us (1%)
    ppermute x14, waiting for transfers between devices, move(): return lax.ppermute(piece, 'wide', [(i, i ^ s) for i in range(wide)])  725 us
    ppermute x14, starting transfers between devices, move(): return lax.ppermute(piece, 'wide', [(i, i ^ s) for i in range(wide)])  282 us
    all_to_all x3, waiting for transfers between devices, exchange(): return lax.all_to_all(send, 'wide', split_axis=0, concat_axis=0, tiled=True)  159 us
    pallas_call x5, Pallas kernels, send_part(): pl.pallas_call(functools.partial(send_kernel, activate), grid=(length //...  118 us
    pallas_call x2, Pallas kernels, back_part(): pl.pallas_call(functools.partial(back_kernel, apart, earlier is not None)...  96.1 us
    pallas_call x4, Pallas kernels, right_part(): pl.pallas_call(functools.partial(right_kernel, apart), grid=(count,), in_...  31.7 us
  transfers between devices with their start and end apart: 32, of which 14 were waited for; matrix products, arithmetic and copies ran while one was open for 0% of the time, Pallas kernels for 17%

profile of v3, /device:TPU:0, one launch (start us, length us, event | category | flops | bytes accessed | tf_op | source)
XLA Modules:
  0.0 1479.7 jit_solution(3108084944626052681)
XLA Ops:
  0.7 8.8 all_gather.6.factor_ref
  9.5 0.8 copy-done
  11.5 3.8 shard_map.77
  15.3 2.6 collective-permute-start
  17.8 1.3 collective-permute-start.1
  19.1 3.6 collective-permute-start.2
  22.9 32.4 %shard_map.78 = bf16[8,16,16,7680]{3,2,1,0:T(8,128)(2,1)} custom-call(bf16[8192,2048]{1,0:T(8,128)(2,1)} %refs_1_.7, bf16[16,8,16,128]{3,2,1,0:T(8,128)(2,1)S(1)} %bitcast.15), custom_call_target="tpu_custom_call" | custom-call | flops 4026531840 | bytes 62914560 | tf_op jit(solution)/shard_map/pallas_call | solution.py:156
  55.3 7.1 all-to-all-start
  63.2 2.0 collective-permute-start.4
  65.1 169.0 %collective-permute-start.5 = (bf16[16,16,512]{2,1,0:T(8,128)(2,1)S(1)}, bf16[16,16,512]{2,1,0:T(8,128)(2,1)S(1)}, u32[]{:S(2)}, u32[]{:S(2)}) collective-permute-start(bf16[16,16,512]{2,1,0:T(8,128)(2,1)S(1)} %get-tuple-element.67), channel_id=1, source_target_pairs={{0,2},{1,3},{2,0},{3,1},{4,6},{5,7},{6,4},{7,5},{8,10},{9,11},{10,... | collective-permute-start | bytes 786440 | tf_op jit(solution)/shard_map/ppermute | solution.py:321
  234.1 6.8 all_gather.7.factor_ref
  241.4 80.7 %collective-permute-done.4.refs_1_ = bf16[16,16,512]{2,1,0:T(8,128)(2,1)S(1)} collective-permute-done((bf16[16,16,512]{2,1,0:T(8,128)(2,1)S(1)}, bf16[16,16,512]{2,1,0:T(8,128)(2,1)S(1)}, u32[]{:S(2)}, u32[]{:S(2)}) %collective-permute-start.4) | collective-permute-done | bytes 262176 | tf_op jit(solution)/shard_map/ppermute | solution.py:321
  322.9 253.0 %collective-permute-done.5.refs_2_ = bf16[16,16,512]{2,1,0:T(8,128)(2,1)S(1)} collective-permute-done((bf16[16,16,512]{2,1,0:T(8,128)(2,1)S(1)}, bf16[16,16,512]{2,1,0:T(8,128)(2,1)S(1)}, u32[]{:S(2)}, u32[]{:S(2)}) %collective-permute-start.5) | collective-permute-done | bytes 262176 | tf_op jit(solution)/shard_map/ppermute | solution.py:321
  576.5 3.6 collective-permute-done.6.refs_3_
  581.7 21.4 %shard_map.80 = (bf16[1,16,8192]{2,1,0:T(8,128)(2,1)S(1)}, bf16[1,16,8192]{2,1,0:T(8,128)(2,1)S(1)}, bf16[1,16,8192]{2,1,0:T(8,128)(2,1)S(1)}, bf16[1,16,8192]{2...) custom-call(bf16[8192,2048]{1,0:T(8,128)(2,1)} %x_ref.9, ...), custom_call_target="tpu_custom_call" | custom-call | flops 268435456 | bytes 35651584 | tf_op jit(solution)/shard_map/pallas_call | solution.py:156
  605.1 9.3 collective-permute-start.7
  614.5 1.0 collective-permute-start.9
  615.5 3.7 collective-permute-start.10
  619.2 39.6 %shard_map.84 = bf16[8,14,16,8192]{3,2,1,0:T(8,128)(2,1)} custom-call(bf16[8192,2048]{1,0:T(8,128)(2,1)} %x_ref.9, bf16[16,8,14,128]{3,2,1,0:T(8,128)(2,1)S(1)} %bitcast.24), custom_call_target="tpu_custom_call" | custom-call | flops 578979823616 | bytes 62914560 | tf_op jit(solution)/shard_map/pallas_call | solution.py:156
  658.8 104.9 %all-to-all-done.refs_0_ = bf16[8,16,16,7680]{3,2,1,0:T(8,128)(2,1)} async-done(((bf16[8,16,16,7680]{3,2,1,0:T(8,128)(2,1)}), bf16[8,16,16,7680]{3,2,1,0:T(8,128)(2,1)}, u32[]{:S(2)}, u32[]{:S(2)}) %all-to-all-start) | async-done | bytes 31457312 | tf_op jit(solution)/shard_map/all_to_all | solution.py:55
  763.7 8.6 all-to-all-start.1
  772.4 87.3 %collective-permute-done.8.refs_5_ = bf16[1,16,8192]{2,1,0:T(8,128)(2,1)} collective-permute-done((bf16[1,16,8192]{2,1,0:T(8,128)(2,1)}, bf16[1,16,8192]{2,1,0:T(8,128)(2,1)}, u32[]{:S(2)}, u32[]{:S(2)}) %collective-permute-start.8) | collective-permute-done | bytes 262176 | tf_op jit(solution)/shard_map/ppermute | solution.py:321
  859.7 8.4 shard_map.81
  868.1 88.9 %collective-permute-start.12 = (bf16[1,16,8192]{2,1,0:T(8,128)(2,1)S(1)}, bf16[1,16,8192]{2,1,0:T(8,128)(2,1)S(1)}, u32[]{:S(2)}, u32[]{:S(2)}) collective-permute-start(bf16[1,16,8192]{2,1,0:T(8,128)(2,1)S(1)} %copy-done.22), channel_id=1, source_target_pairs={{0,2},{1,3},{2,0},{3,1},{4,6},{5,7},{6,4},{7,5},{8,10},{9,11},{10,... | collective-permute-start | bytes 786440 | tf_op jit(solution)/shard_map/ppermute | solution.py:321
  957.1 57.7 %collective-permute-done.11.refs_1_ = bf16[1,16,8192]{2,1,0:T(8,128)(2,1)S(1)} collective-permute-done((bf16[1,16,8192]{2,1,0:T(8,128)(2,1)S(1)}, bf16[1,16,8192]{2,1,0:T(8,128)(2,1)S(1)}, u32[]{:S(2)}, u32[]{:S(2)}) %collective-permute-start.11) | collective-permute-done | bytes 262176 | tf_op jit(solution)/shard_map/ppermute | solution.py:321
  1014.8 238.3 %collective-permute-done.12.refs_2_ = bf16[1,16,8192]{2,1,0:T(8,128)(2,1)S(1)} collective-permute-done((bf16[1,16,8192]{2,1,0:T(8,128)(2,1)S(1)}, bf16[1,16,8192]{2,1,0:T(8,128)(2,1)S(1)}, u32[]{:S(2)}, u32[]{:S(2)}) %collective-permute-start.12) | collective-permute-done | bytes 262176 | tf_op jit(solution)/shard_map/ppermute | solution.py:321
  1253.2 4.7 collective-permute-done.13.refs_3_
  1257.8 87.7 %shard_map.82 = (bf16[8192,2048]{1,0:T(8,128)(2,1)}, f32[16,128,128]{2,1,0:T(8,128)S(1)}) custom-call(bf16[8,16,16,7680]{3,2,1,0:T(8,128)(2,1)} %all-to-all-done.refs_0_, bf16[8192,2048]{1,0:T(8,128)(2,1)} %x_ref.9, bf16[16,128,128]{2,1,0:T(8,128)(2,1)S(1)} %shard_map.79.refs_9_.refs_2_, ...), custom_call_target="tpu_custom_call", output_to_operand_aliasing={{0}: (3, {})} | custom-call | flops 504323112960 | bytes 94371840 | tf_op jit(solution)/shard_map/pallas_call | solution.py:282
  1345.6 1.2 shard_map.83
  1346.8 1.2 collective-permute-start.15
  1348.7 21.3 %shard_map.88 = bf16[8,1,16,8192]{3,2,1,0:T(8,128)(2,1)} custom-call(bf16[8192,2048]{1,0:T(8,128)(2,1)} %x_ref.9, bf16[16,8,1,128]{3,2,1,0:T(2,128)(2,1)S(1)} %get-tuple-element.111.w_ref), custom_call_target="tpu_custom_call" | custom-call | flops 268435456 | bytes 35651584 | tf_op jit(solution)/shard_map/pallas_call | solution.py:156
  1370.0 0.8 add_add_fusion
  1370.8 43.2 %all-to-all-done.1.refs_0_ = bf16[8,14,16,8192]{3,2,1,0:T(8,128)(2,1)} async-done(((bf16[8,14,16,8192]{3,2,1,0:T(8,128)(2,1)}), bf16[8,14,16,8192]{3,2,1,0:T(8,128)(2,1)}, u32[]{:S(2)}, u32[]{:S(2)}) %all-to-all-start.1) | async-done | bytes 29360160 | tf_op jit(solution)/shard_map/all_to_all | solution.py:55
  1414.0 10.0 all-to-all-start.2
  1424.1 2.9 shard_map.87
  1427.5 0.9 collective-permute-start.24
  1428.9 1.4 collective-permute-done.25
  1430.3 0.9 collective-permute-done.24
  1431.3 13.2 shard_map.86
  1444.9 1.1 collective-permute-start.21
  1446.4 13.1 shard_map.85
  1459.5 0.8 collective-permute-start.19
  1460.3 1.1 collective-permute-start.18
  1461.5 11.0 all-to-all-done.2.refs_0_
  1472.5 2.5 shard_map.89
  1475.1 1.2 collective-permute-start.27
  1477.0 1.3 collective-permute-done.28
  1479.0 0.7 pad_maximum_fusion
  (100 shorter events, 11.9 us)
Async XLA Ops:
  15.3 47.2 %collective-permute-start = (bf16[16,16,512]{2,1,0:T(8,128)(2,1)}, bf16[16,16,512]{2,1,0:T(8,128)(2,1)S(1)}, u32[]{:S(2)}, u32[]{:S(2)}) collective-permute-start(bf16[16,16,512]{2,1,0:T(8,128)(2,1)} %get-tuple-element.59), channel_id=1, source_target_pairs={{0,4},{1,5},{2,6},{3,7},{4,0},{5,1},{6,2},{7,3},{8,12},{9,13},{10,... | collective-permute-start | bytes 786440 | tf_op jit(solution)/shard_map/ppermute | solution.py:321
  17.8 45.3 %collective-permute-start.1 = (bf16[16,16,512]{2,1,0:T(8,128)(2,1)S(1)}, bf16[16,16,512]{2,1,0:T(8,128)(2,1)S(1)}, u32[]{:S(2)}, u32[]{:S(2)}) collective-permute-start(bf16[16,16,512]{2,1,0:T(8,128)(2,1)S(1)} %get-tuple-element.60), channel_id=1, source_target_pairs={{0,5},{1,4},{2,7},{3,6},{4,1},{5,0},{6,3},{7,2},{8,13},{9,12},{10,... | collective-permute-start | bytes 786440 | tf_op jit(solution)/shard_map/ppermute | solution.py:321
  19.1 44.0 %collective-permute-start.2 = (bf16[16,16,512]{2,1,0:T(8,128)(2,1)S(1)}, bf16[16,16,512]{2,1,0:T(8,128)(2,1)S(1)}, u32[]{:S(2)}, u32[]{:S(2)}) collective-permute-start(bf16[16,16,512]{2,1,0:T(8,128)(2,1)S(1)} %get-tuple-element.61), channel_id=1, source_target_pairs={{0,6},{1,7},{2,4},{3,5},{4,2},{5,3},{6,0},{7,1},{8,14},{9,15},{10,... | collective-permute-start | bytes 786440 | tf_op jit(solution)/shard_map/ppermute | solution.py:321
  22.7 40.4 %collective-permute-start.3 = (bf16[16,16,512]{2,1,0:T(8,128)(2,1)S(1)}, bf16[16,16,512]{2,1,0:T(8,128)(2,1)S(1)}, u32[]{:S(2)}, u32[]{:S(2)}) collective-permute-start(bf16[16,16,512]{2,1,0:T(8,128)(2,1)S(1)} %get-tuple-element.62), channel_id=1, source_target_pairs={{0,7},{1,6},{2,5},{3,4},{4,3},{5,2},{6,1},{7,0},{8,15},{9,14},{10,... | collective-permute-start | bytes 786440 | tf_op jit(solution)/shard_map/ppermute | solution.py:321
  55.3 178.8 %copy-start.25 = (bf16[16,32,128]{2,1,0:T(8,128)(2,1)S(1)}, bf16[16,32,128]{2,1,0:T(8,128)(2,1)}, u32[]{:S(2)}) copy-start(bf16[16,32,128]{2,1,0:T(8,128)(2,1)} %param.7) | copy-start | bytes 393220
  55.3 185.6 %copy-start.1 = (s32[16384]{0:T(1024)S(1)}, s32[16384]{0:T(1024)}, u32[]{:S(2)}) copy-start(s32[16384]{0:T(1024)} %param.9) | copy-start | bytes 196612
  55.3 708.4 %all-to-all-start = ((bf16[8,16,16,7680]{3,2,1,0:T(8,128)(2,1)}), bf16[8,16,16,7680]{3,2,1,0:T(8,128)(2,1)}, u32[]{:S(2)}, u32[]{:S(2)}) async-start(bf16[8,16,16,7680]{3,2,1,0:T(8,128)(2,1)} %shard_map.78), calls=%async_computation | async-start | bytes 62914560 | tf_op jit(solution)/shard_map/all_to_all | solution.py:55
  63.2 556.0 %copy-start.11 = (bf16[16,16,512]{2,1,0:T(8,128)(2,1)}, bf16[16,16,512]{2,1,0:T(8,128)(2,1)S(1)}, u32[]{:S(2)}) copy-start(bf16[16,16,512]{2,1,0:T(8,128)(2,1)S(1)} %collective-permute-done.3.refs_7_) | copy-start | bytes 786436
  63.2 259.0 %collective-permute-start.4 = (bf16[16,16,512]{2,1,0:T(8,128)(2,1)S(1)}, bf16[16,16,512]{2,1,0:T(8,128)(2,1)S(1)}, u32[]{:S(2)}, u32[]{:S(2)}) collective-permute-start(bf16[16,16,512]{2,1,0:T(8,128)(2,1)S(1)} %get-tuple-element.65), channel_id=1, source_target_pairs={{0,1},{1,0},{2,3},{3,2},{4,5},{5,4},{6,7},{7,6},{8,9},{9,8},{10,11... | collective-permute-start | bytes 786440 | tf_op jit(solution)/shard_map/ppermute | solution.py:321
  65.1 510.7 %collective-permute-start.5 = (bf16[16,16,512]{2,1,0:T(8,128)(2,1)S(1)}, bf16[16,16,512]{2,1,0:T(8,128)(2,1)S(1)}, u32[]{:S(2)}, u32[]{:S(2)}) collective-permute-start(bf16[16,16,512]{2,1,0:T(8,128)(2,1)S(1)} %get-tuple-element.67), channel_id=1, source_target_pairs={{0,2},{1,3},{2,0},{3,1},{4,6},{5,7},{6,4},{7,5},{8,10},{9,11},{10,... | collective-permute-start | bytes 786440 | tf_op jit(solution)/shard_map/ppermute | solution.py:321
  234.1 346.0 %collective-permute-start.6 = (bf16[16,16,512]{2,1,0:T(8,128)(2,1)S(1)}, bf16[16,16,512]{2,1,0:T(8,128)(2,1)S(1)}, u32[]{:S(2)}, u32[]{:S(2)}) collective-permute-start(bf16[16,16,512]{2,1,0:T(8,128)(2,1)S(1)} %get-tuple-element.69), channel_id=1, source_target_pairs={{0,3},{1,2},{2,1},{3,0},{4,7},{5,6},{6,5},{7,4},{8,11},{9,10},{10,... | collective-permute-start | bytes 786440 | tf_op jit(solution)/shard_map/ppermute | solution.py:321
  605.1 167.2 %collective-permute-start.7 = (bf16[1,16,8192]{2,1,0:T(8,128)(2,1)}, bf16[1,16,8192]{2,1,0:T(8,128)(2,1)}, u32[]{:S(2)}, u32[]{:S(2)}) collective-permute-start(bf16[1,16,8192]{2,1,0:T(8,128)(2,1)} %get-tuple-element.71), channel_id=1, source_target_pairs={{0,4},{1,5},{2,6},{3,7},{4,0},{5,1},{6,2},{7,3},{8,12},{9,13},{10,... | collective-permute-start | bytes 786440 | tf_op jit(solution)/shard_map/ppermute | solution.py:321
  614.5 245.2 %collective-permute-start.8 = (bf16[1,16,8192]{2,1,0:T(8,128)(2,1)}, bf16[1,16,8192]{2,1,0:T(8,128)(2,1)}, u32[]{:S(2)}, u32[]{:S(2)}) collective-permute-start(bf16[1,16,8192]{2,1,0:T(8,128)(2,1)} %get-tuple-element.72), channel_id=1, source_target_pairs={{0,5},{1,4},{2,7},{3,6},{4,1},{5,0},{6,3},{7,2},{8,13},{9,12},{10,... | collective-permute-start | bytes 786440 | tf_op jit(solution)/shard_map/ppermute | solution.py:321
  614.5 245.2 %collective-permute-start.9 = (bf16[1,16,8192]{2,1,0:T(8,128)(2,1)}, bf16[1,16,8192]{2,1,0:T(8,128)(2,1)}, u32[]{:S(2)}, u32[]{:S(2)}) collective-permute-start(bf16[1,16,8192]{2,1,0:T(8,128)(2,1)} %get-tuple-element.73), channel_id=1, source_target_pairs={{0,6},{1,7},{2,4},{3,5},{4,2},{5,3},{6,0},{7,1},{8,14},{9,15},{10,... | collective-permute-start | bytes 786440 | tf_op jit(solution)/shard_map/ppermute | solution.py:321
  615.5 244.1 %collective-permute-start.10 = (bf16[1,16,8192]{2,1,0:T(8,128)(2,1)}, bf16[1,16,8192]{2,1,0:T(8,128)(2,1)}, u32[]{:S(2)}, u32[]{:S(2)}) collective-permute-start(bf16[1,16,8192]{2,1,0:T(8,128)(2,1)} %get-tuple-element.74), channel_id=1, source_target_pairs={{0,7},{1,6},{2,5},{3,4},{4,3},{5,2},{6,1},{7,0},{8,15},{9,14},{10,... | collective-permute-start | bytes 786440 | tf_op jit(solution)/shard_map/ppermute | solution.py:321
  658.8 200.8 %copy-start.10 = (bf16[16,16,512]{2,1,0:T(8,128)(2,1)S(1)}, bf16[16,16,512]{2,1,0:T(8,128)(2,1)}, u32[]{:S(2)}) copy-start(bf16[16,16,512]{2,1,0:T(8,128)(2,1)} %copy-done.9) | copy-start | bytes 786436
  658.8 200.8 %copy-start.12 = (bf16[16,16,512]{2,1,0:T(8,128)(2,1)S(1)}, bf16[16,16,512]{2,1,0:T(8,128)(2,1)}, u32[]{:S(2)}) copy-start(bf16[16,16,512]{2,1,0:T(8,128)(2,1)} %copy-done.11) | copy-start | bytes 786436
  658.8 200.8 %copy-start.14 = (bf16[16,16,512]{2,1,0:T(8,128)(2,1)S(1)}, bf16[16,16,512]{2,1,0:T(8,128)(2,1)}, u32[]{:S(2)}) copy-start(bf16[16,16,512]{2,1,0:T(8,128)(2,1)} %copy-done.13) | copy-start | bytes 786436
  658.8 200.9 %copy-start.16 = (bf16[16,16,512]{2,1,0:T(8,128)(2,1)S(1)}, bf16[16,16,512]{2,1,0:T(8,128)(2,1)}, u32[]{:S(2)}) copy-start(bf16[16,16,512]{2,1,0:T(8,128)(2,1)} %copy-done.15) | copy-start | bytes 786436
  658.8 200.9 %copy-start.18 = (bf16[16,16,512]{2,1,0:T(8,128)(2,1)S(1)}, bf16[16,16,512]{2,1,0:T(8,128)(2,1)}, u32[]{:S(2)}) copy-start(bf16[16,16,512]{2,1,0:T(8,128)(2,1)} %copy-done.17) | copy-start | bytes 786436
  763.7 650.3 %all-to-all-start.1 = ((bf16[8,14,16,8192]{3,2,1,0:T(8,128)(2,1)}), bf16[8,14,16,8192]{3,2,1,0:T(8,128)(2,1)}, u32[]{:S(2)}, u32[]{:S(2)}) async-start(bf16[8,14,16,8192]{3,2,1,0:T(8,128)(2,1)} %shard_map.84), calls=%async_computation.1 | async-start | bytes 58720256 | tf_op jit(solution)/shard_map/all_to_all | solution.py:55
  772.3 95.8 %copy-start.24 = (bf16[1,16,8192]{2,1,0:T(8,128)(2,1)S(1)}, bf16[1,16,8192]{2,1,0:T(8,128)(2,1)}, u32[]{:S(2)}) copy-start(bf16[1,16,8192]{2,1,0:T(8,128)(2,1)} %copy-done.23) | copy-start | bytes 786436
  772.3 95.8 %copy-start.22 = (bf16[1,16,8192]{2,1,0:T(8,128)(2,1)S(1)}, bf16[1,16,8192]{2,1,0:T(8,128)(2,1)}, u32[]{:S(2)}) copy-start(bf16[1,16,8192]{2,1,0:T(8,128)(2,1)} %copy-done.21) | copy-start | bytes 786436
  772.3 184.8 %copy-start.20 = (bf16[1,16,8192]{2,1,0:T(8,128)(2,1)S(1)}, bf16[1,16,8192]{2,1,0:T(8,128)(2,1)}, u32[]{:S(2)}) copy-start(bf16[1,16,8192]{2,1,0:T(8,128)(2,1)} %copy-done.19) | copy-start | bytes 786436
  868.1 146.7 %collective-permute-start.11 = (bf16[1,16,8192]{2,1,0:T(8,128)(2,1)S(1)}, bf16[1,16,8192]{2,1,0:T(8,128)(2,1)S(1)}, u32[]{:S(2)}, u32[]{:S(2)}) collective-permute-start(bf16[1,16,8192]{2,1,0:T(8,128)(2,1)S(1)} %copy-done.24), channel_id=1, source_target_pairs={{0,1},{1,0},{2,3},{3,2},{4,5},{5,4},{6,7},{7,6},{8,9},{9,8},{10,11... | collective-permute-start | bytes 786440 | tf_op jit(solution)/shard_map/ppermute | solution.py:321
  868.1 385.0 %collective-permute-start.12 = (bf16[1,16,8192]{2,1,0:T(8,128)(2,1)S(1)}, bf16[1,16,8192]{2,1,0:T(8,128)(2,1)S(1)}, u32[]{:S(2)}, u32[]{:S(2)}) collective-permute-start(bf16[1,16,8192]{2,1,0:T(8,128)(2,1)S(1)} %copy-done.22), channel_id=1, source_target_pairs={{0,2},{1,3},{2,0},{3,1},{4,6},{5,7},{6,4},{7,5},{8,10},{9,11},{10,... | collective-permute-start | bytes 786440 | tf_op jit(solution)/shard_map/ppermute | solution.py:321
  957.1 300.7 %collective-permute-start.13 = (bf16[1,16,8192]{2,1,0:T(8,128)(2,1)S(1)}, bf16[1,16,8192]{2,1,0:T(8,128)(2,1)S(1)}, u32[]{:S(2)}, u32[]{:S(2)}) collective-permute-start(bf16[1,16,8192]{2,1,0:T(8,128)(2,1)S(1)} %copy-done.20), channel_id=1, source_target_pairs={{0,3},{1,2},{2,1},{3,0},{4,7},{5,6},{6,5},{7,4},{8,11},{9,10},{10,... | collective-permute-start | bytes 786440 | tf_op jit(solution)/shard_map/ppermute | solution.py:321
  1014.8 330.7 %copy-start.3 = (bf16[1,16,8192]{2,1,0:T(8,128)(2,1)}, bf16[1,16,8192]{2,1,0:T(8,128)(2,1)S(1)}, u32[]{:S(2)}) copy-start(bf16[1,16,8192]{2,1,0:T(8,128)(2,1)S(1)} %collective-permute-done.11.refs_1_) | copy-start | bytes 786436
  1253.2 92.4 %copy-start.5 = (bf16[1,16,8192]{2,1,0:T(8,128)(2,1)}, bf16[1,16,8192]{2,1,0:T(8,128)(2,1)S(1)}, u32[]{:S(2)}) copy-start(bf16[1,16,8192]{2,1,0:T(8,128)(2,1)S(1)} %collective-permute-done.12.refs_2_) | copy-start | bytes 786436
  1257.8 87.7 %copy-start.7 = (bf16[1,16,8192]{2,1,0:T(8,128)(2,1)}, bf16[1,16,8192]{2,1,0:T(8,128)(2,1)S(1)}, u32[]{:S(2)}) copy-start(bf16[1,16,8192]{2,1,0:T(8,128)(2,1)S(1)} %collective-permute-done.13.refs_3_) | copy-start | bytes 786436
  1345.5 78.5 %copy-start.2 = (s32[16384]{0:T(1024)S(1)}, s32[16384]{0:T(1024)}, u32[]{:S(2)}) copy-start(s32[16384]{0:T(1024)} %param.9) | copy-start | bytes 196612
  1345.5 78.5 %copy-start.4 = (bf16[1,16,8192]{2,1,0:T(8,128)(2,1)S(1)}, bf16[1,16,8192]{2,1,0:T(8,128)(2,1)}, u32[]{:S(2)}) copy-start(bf16[1,16,8192]{2,1,0:T(8,128)(2,1)} %copy-done.3) | copy-start | bytes 786436
  1346.7 23.3 %collective-permute-start.16 = (f32[16,32,128]{2,1,0:T(8,128)S(1)}, f32[16,32,128]{2,1,0:T(8,128)S(1)}, u32[]{:S(2)}, u32[]{:S(2)}) collective-permute-start(f32[16,32,128]{2,1,0:T(8,128)S(1)} %get-tuple-element.90), channel_id=1, source_target_pairs={{0,24},{8,16},{16,8},{24,0},{1,25},{9,17},{17,9},{25,1},{2,26},{10... | collective-permute-start | bytes 786440 | tf_op jit(solution)/shard_map/ppermute | solution.py:303
  1346.8 23.2 %collective-permute-start.15 = (f32[16,32,128]{2,1,0:T(8,128)S(1)}, f32[16,32,128]{2,1,0:T(8,128)S(1)}, u32[]{:S(2)}, u32[]{:S(2)}) collective-permute-start(f32[16,32,128]{2,1,0:T(8,128)S(1)} %get-tuple-element.89), channel_id=1, source_target_pairs={{0,16},{8,24},{16,0},{24,8},{1,17},{9,25},{17,1},{25,9},{2,18},{10... | collective-permute-start | bytes 786440 | tf_op jit(solution)/shard_map/ppermute | solution.py:303
  1348.0 22.0 %collective-permute-start.14 = (f32[16,32,128]{2,1,0:T(8,128)S(1)}, f32[16,32,128]{2,1,0:T(8,128)S(1)}, u32[]{:S(2)}, u32[]{:S(2)}) collective-permute-start(f32[16,32,128]{2,1,0:T(8,128)S(1)} %get-tuple-element.88), channel_id=1, source_target_pairs={{0,8},{8,0},{16,24},{24,16},{1,9},{9,1},{17,25},{25,17},{2,10},{10... | collective-permute-start | bytes 786440 | tf_op jit(solution)/shard_map/ppermute | solution.py:303
  1414.0 58.5 %all-to-all-start.2 = ((bf16[8,1,16,8192]{3,2,1,0:T(8,128)(2,1)}), bf16[8,1,16,8192]{3,2,1,0:T(8,128)(2,1)S(1)}, u32[]{:S(2)}, u32[]{:S(2)}) async-start(bf16[8,1,16,8192]{3,2,1,0:T(8,128)(2,1)} %shard_map.88), calls=%async_computation.2 | async-start | bytes 4194304 | tf_op jit(solution)/shard_map/all_to_all | solution.py:55
  1427.0 3.4 collective-permute-start.25
  1427.5 3.7 collective-permute-start.24
  1428.5 2.8 collective-permute-start.23
  1444.4 16.9 %collective-permute-start.22 = (f32[7,32,128]{2,1,0:T(8,128)S(1)}, f32[7,32,128]{2,1,0:T(8,128)S(1)}, u32[]{:S(2)}, u32[]{:S(2)}) collective-permute-start(f32[7,32,128]{2,1,0:T(8,128)S(1)} %get-tuple-element.101), channel_id=1, source_target_pairs={{0,24},{8,16},{16,8},{24,0},{1,25},{9,17},{17,9},{25,1},{2,26},{10... | collective-permute-start | bytes 344072 | tf_op jit(solution)/shard_map/ppermute | solution.py:303
  1444.9 16.5 %collective-permute-start.21 = (f32[7,32,128]{2,1,0:T(8,128)S(1)}, f32[7,32,128]{2,1,0:T(8,128)S(1)}, u32[]{:S(2)}, u32[]{:S(2)}) collective-permute-start(f32[7,32,128]{2,1,0:T(8,128)S(1)} %get-tuple-element.100), channel_id=1, source_target_pairs={{0,16},{8,24},{16,0},{24,8},{1,17},{9,25},{17,1},{25,9},{2,18},{10... | collective-permute-start | bytes 344072 | tf_op jit(solution)/shard_map/ppermute | solution.py:303
  1446.0 15.4 %collective-permute-start.20 = (f32[7,32,128]{2,1,0:T(8,128)S(1)}, f32[7,32,128]{2,1,0:T(8,128)S(1)}, u32[]{:S(2)}, u32[]{:S(2)}) collective-permute-start(f32[7,32,128]{2,1,0:T(8,128)S(1)} %get-tuple-element.99), channel_id=1, source_target_pairs={{0,8},{8,0},{16,24},{24,16},{1,9},{9,1},{17,25},{25,17},{2,10},{10... | collective-permute-start | bytes 344072 | tf_op jit(solution)/shard_map/ppermute | solution.py:303
  1459.5 16.8 %collective-permute-start.19 = (f32[7,32,128]{2,1,0:T(8,128)S(1)}, f32[7,32,128]{2,1,0:T(8,128)S(1)}, u32[]{:S(2)}, u32[]{:S(2)}) collective-permute-start(f32[7,32,128]{2,1,0:T(8,128)S(1)} %get-tuple-element.97), channel_id=1, source_target_pairs={{0,24},{8,16},{16,8},{24,0},{1,25},{9,17},{17,9},{25,1},{2,26},{10... | collective-permute-start | bytes 344072 | tf_op jit(solution)/shard_map/ppermute | solution.py:303
  1460.3 16.7 %collective-permute-start.18 = (f32[7,32,128]{2,1,0:T(8,128)S(1)}, f32[7,32,128]{2,1,0:T(8,128)S(1)}, u32[]{:S(2)}, u32[]{:S(2)}) collective-permute-start(f32[7,32,128]{2,1,0:T(8,128)S(1)} %get-tuple-element.96), channel_id=1, source_target_pairs={{0,16},{8,24},{16,0},{24,8},{1,17},{9,25},{17,1},{25,9},{2,18},{10... | collective-permute-start | bytes 344072 | tf_op jit(solution)/shard_map/ppermute | solution.py:303
  1461.4 15.6 %collective-permute-start.17 = (f32[7,32,128]{2,1,0:T(8,128)S(1)}, f32[7,32,128]{2,1,0:T(8,128)S(1)}, u32[]{:S(2)}, u32[]{:S(2)}) collective-permute-start(f32[7,32,128]{2,1,0:T(8,128)S(1)} %get-tuple-element.95), channel_id=1, source_target_pairs={{0,8},{8,0},{16,24},{24,16},{1,9},{9,1},{17,25},{25,17},{2,10},{10... | collective-permute-start | bytes 344072 | tf_op jit(solution)/shard_map/ppermute | solution.py:303
  1475.1 3.2 collective-permute-start.28
  1475.1 3.8 collective-permute-start.27
  1476.3 2.6 collective-permute-start.26
  (10 other events, 162.8 us)
